TPU v7x, 256 devices: a whole 4x4x8 slice. The times are simulated.
256 devices in a mesh: dp: 8 (over z_lo, x), dap: 32 (over y, z_hi, core).
Axes of the slice: x: 4, y: 4, z: 8 (z_hi: 4, z_lo: 2; z = z_hi * 2 + z_lo), core: 2. Of those that a mesh axis runs over, the one named last changes fastest.
Arguments:
- pair: float32 [8, 192, 192, 128], P('dp', 'dap'), may hold values from -6 to 6
- upstream: float32 [8, 192, 192, 128], P('dp', 'dap'), may hold values from -6 to 6
- residue_mask: int32 [8, 192], P('dp'), may hold values 0 or 1
- w_in: float32 [128, 512], replicated, may hold values from -0.5 to 0.5
- w_gate: float32 [128, 128], replicated, may hold values from -0.5 to 0.5
- w_out: float32 [128, 128], replicated, may hold values from -0.5 to 0.5
- gains: float32 [2, 128], replicated, may hold values from 0.5 to 1.5
Outputs:
- d_pair: float32 [8, 192, 192, 128], P('dp', 'dap')
- d_w_in: float32 [128, 512], replicated
- d_w_gate: float32 [128, 128], replicated
- d_w_out: float32 [128, 128], replicated
- d_gains: float32 [2, 128], replicated
All inputs are finite; a program needn't handle non-finite values. No bound on the sum of `residue_mask` on one device may be relied on, other than what follows from the above.
Results may differ from a plain program's by a relative error of at most 0.000082.
Values sent between devices are 32-bit elements; how exact they have to be, the bound alone decides.
No kernel may reach another device: no remote copies, remote signals or barrier semaphores. Data moves between devices by JAX's collectives and lax.ppermute only.
A program may use at most 192 MiB of HBM per device.

v0:
```python
import jax
import jax.numpy as jnp
from jax import lax
from jax.sharding import PartitionSpec as P

HIGH = lax.Precision.HIGHEST


def layer_norm_backward(grad_hat, normal, inverse):
    first = jnp.mean(grad_hat, axis=-1, keepdims=True)
    second = jnp.mean(grad_hat * normal, axis=-1, keepdims=True)
    return inverse * (grad_hat - first - normal * second)


def standard_layer_norm(values):
    center = values - jnp.mean(values, axis=-1, keepdims=True)
    inverse = lax.rsqrt(jnp.mean(center * center, axis=-1, keepdims=True) + 1e-05)
    return (center * inverse, inverse)


def shards(pair, upstream, residue_mask, w_in, w_gate, w_out, gains):
    width = w_out.shape[0]
    rows = pair.shape[1]
    first_row = lax.axis_index("dap") * rows
    maskf = residue_mask.astype(jnp.float32)
    row_mask = lax.dynamic_slice_in_dim(maskf, first_row, rows, 1)
    pairmask = (row_mask[:, :, None] * maskf[:, None, :])[..., None]
    zhat, z_inv = standard_layer_norm(pair)
    zn = zhat * gains[0]
    proj = jnp.einsum("sijc,cf->sijf", zn, w_in, precision=HIGH)
    a_proj = proj[..., :width]
    a_sig = jax.nn.sigmoid(proj[..., width : 2 * width])
    b_proj = proj[..., 2 * width : 3 * width]
    b_sig = jax.nn.sigmoid(proj[..., 3 * width :])
    a_val = pairmask * a_sig * a_proj
    b_val = pairmask * b_sig * b_proj
    b_whole = lax.all_gather(b_val, "dap", axis=1, tiled=True)
    triangle_product = jnp.einsum("sikh,sjkh->sijh", a_val, b_whole, precision=HIGH)
    input_centered_scaled, input_inverse_stddev = standard_layer_norm(triangle_product)
    normed_input = input_centered_scaled * gains[1]
    proj_out = jnp.einsum("sijh,hc->sijc", normed_input, w_out, precision=HIGH)
    gate = jax.nn.sigmoid(jnp.einsum("sijc,cd->sijd", zn, w_gate, precision=HIGH))
    d_gate_logit = upstream * proj_out * gate * (1.0 - gate)
    d_proj_out = upstream * gate
    grad_w_out = jnp.einsum("sijh,sijc->hc", normed_input, d_proj_out, precision=HIGH)
    normed_input_gradient = jnp.einsum("sijc,hc->sijh", d_proj_out, w_out, precision=HIGH)
    output_gain_gradient = jnp.sum(normed_input_gradient * input_centered_scaled, axis=(0, 1, 2))
    triangle_gradient = layer_norm_backward(
        normed_input_gradient * gains[1], input_centered_scaled, input_inverse_stddev
    )
    d_a = jnp.einsum("sijh,sjkh->sikh", triangle_gradient, b_whole, precision=HIGH)
    d_b = jnp.transpose(
        lax.psum_scatter(
            jnp.einsum("sijh,sikh->jskh", triangle_gradient, a_val, precision=HIGH),
            "dap",
            scatter_dimension=0,
            tiled=True,
        ),
        (1, 0, 2, 3),
    )
    d_a_masked = d_a * pairmask
    d_b_masked = d_b * pairmask
    d_proj = jnp.concatenate(
        [
            d_a_masked * a_sig,
            d_a_masked * a_proj * a_sig * (1.0 - a_sig),
            d_b_masked * b_sig,
            d_b_masked * b_proj * b_sig * (1.0 - b_sig),
        ],
        axis=-1,
    )
    grad_w_in = jnp.einsum("sijc,sijf->cf", zn, d_proj, precision=HIGH)
    grad_w_gate = jnp.einsum("sijc,sijd->cd", zn, d_gate_logit, precision=HIGH)
    d_zn = jnp.einsum("sijf,cf->sijc", d_proj, w_in, precision=HIGH)
    d_zn = d_zn + jnp.einsum("sijd,cd->sijc", d_gate_logit, w_gate, precision=HIGH)
    grad_gain_in = jnp.sum(d_zn * zhat, axis=(0, 1, 2))
    d_pair = layer_norm_backward(d_zn * gains[0], zhat, z_inv)
    grad_gains = jnp.stack([grad_gain_in, output_gain_gradient], axis=0)
    total_in, total_gate, total_out, total_gains = lax.psum(
        (grad_w_in, grad_w_gate, grad_w_out, grad_gains), ("dp", "dap")
    )
    return (d_pair, total_in, total_gate, total_out, total_gains)


def solution(mesh):
    in_specs = (
        P("dp", "dap", None, None),
        P("dp", "dap", None, None),
        P("dp", None),
        P(),
        P(),
        P(),
        P(),
    )
    out_specs = (P("dp", "dap", None, None), P(), P(), P(), P())
    return jax.shard_map(shards, mesh=mesh, in_specs=in_specs, out_specs=out_specs, check_vma=False)
```

profile of v0, /device:TPU:1, one launch (start us, length us, event | category | flops | bytes accessed | tf_op | source)
XLA Modules:
  0.0 769.3 jit_solution(12633627629797848918)
XLA Ops:
  7.2 0.0 copy-start
  7.2 0.0 all-gather.2.cloned.1.call-start
  7.2 0.7 convert_element_type.3
  7.9 0.8 slice_bitcast_fusion
  8.7 1.3 reduce_sum.90
  10.1 1.5 multiply_reduce_fusion.2
  11.6 0.0 copy-start.19
  11.6 0.1 dynamic-slice_bitcast_fusion
  11.7 0.1 broadcast_multiply_fusion
  11.8 3.1 convolution_bitcast_fusion
  15.0 1.4 copy-done.1
  16.4 1.2 multiply_bitcast_fusion.2
  17.6 0.0 copy-done.23
  17.6 0.0 all-gather.2.cloned.1.call-update
  17.6 0.2 reduce-scatter.2.cloned.1.call-start
  17.8 0.0 copy-done.29
  17.8 0.0 copy-done.19
  17.9 0.0 copy-done.3
  17.9 0.0 copy-done.25
  17.9 0.8 fusion.12
  18.7 0.8 copy-done.7
  19.5 1.4 fusion.34
  21.0 1.5 copy.25
  22.5 1.4 copy.24
  23.9 0.2 multiply_reduce_fusion.1
  24.1 0.6 broadcast_multiply_fusion.4
  24.7 115.0 %all-gather.2.cloned.1.call-done = f32[1,192,192,128]{3,2,0,1:T(8,128)} async-done(((f32[1,6,192,128]{3,2,0,1:T(8,128)}), f32[1,192,192,128]{3,2,0,1:T(8,128)}) %all-gather.2.cloned.1.call-update) | async-done | bytes 18874384 | tf_op jit(solution)/shard_map/all_gather | solution.py:37
  139.7 24.8 %copy.23 = f32[1,192,192,128]{2,1,3,0:T(8,128)} copy(f32[1,192,192,128]{3,2,0,1:T(8,128)} %all-gather.2.cloned.1.call-done) | data formatting | bytes 37748736 | tf_op jit(solution)/shard_map/all_gather | solution.py:37
  164.5 25.2 %fusion.61 = (f32[6,192]{1,0:T(8,128)S(1)}, f32[1,6,192,128]{2,1,3,0:T(8,128)S(1)}) fusion(f32[6,192,128]{1,0,2:T(8,128)} %copy.24, f32[1,192,192,128]{2,1,3,0:T(8,128)} %copy.23), kind=kOutput, calls=%fused_computation.98 | convolution fusion | flops 339884928 | bytes 20058624 | tf_op jit(solution)/shard_map/sikh,sjkh->sijh/dot_general | solution.py:38
  189.7 0.0 copy-start.4
  189.8 0.0 copy-start.21
  189.8 0.2 multiply_reduce_fusion
  190.0 0.0 copy-start.18
  190.0 2.7 fusion.18
  192.8 0.6 copy-done.22
  193.4 24.0 %fusion.19 = f32[128,192,192]{2,1,0:T(8,128)} fusion(f32[6,192,128]{1,0,2:T(8,128)S(1)} %copy-done.4, f32[6,192,128]{1,0,2:T(8,128)S(1)} %copy.25, f32[1,6,192,128]{2,1,3,0:T(8,128)S(1)} %get-tuple-element.24, f32[6,192]{1,0:T(8,128)S(1)} %broadcast_multiply_fusion.3, f32[6,192]{1,0:T(8,128)S(1)} %copy-done.21, f32[128]{0:T(128)S(1)} %copy-done.28, ...), kind=kOutput, calls=%fused_computation.24 | convolution fusion | flops 340770816 | bytes 20662784 | tf_op jit(solution)/shard_map/sijh,sikh->jskh/dot_general | solution.py:54
  217.4 23.2 %copy.28 = f32[128,192,192]{0,1,2:T(8,128)} copy(f32[128,192,192]{2,1,0:T(8,128)} %fusion.19) | data formatting | bytes 37748736 | tf_op jit(solution)/shard_map/sijh,sikh->jskh/dot_general | solution.py:54
  240.6 0.0 reduce-scatter.2.cloned.1.call-update
  240.6 0.0 all-reduce.3.cloned.1.call-start
  240.7 17.8 %fusion = f32[128,192,6]{1,2,0:T(8,128)} fusion(f32[1,192,192,128]{2,1,3,0:T(8,128)} %copy.23, f32[6,192,128]{1,0,2:T(8,128)S(1)} %copy.25, f32[1,6,192,128]{2,1,3,0:T(8,128)S(1)} %get-tuple-element.24, f32[6,192]{1,0:T(8,128)} %copy-done.22, f32[6,192]{1,0:T(8,128)} %broadcast_multiply_fusion.4, f32[128]{0:T(128)} %copy-done.27, f32[6,192]{1,0:T(8,128)} %copy-done.18, ...), kind=kOutput, calls=%fused_computation | convolution fusion | flops 340770816 | bytes 20662784 | tf_op jit(solution)/shard_map/sijh,sjkh->sikh/dot_general | solution.py:51
  258.5 2.4 copy.26
  260.9 1.6 copy.29
  262.5 0.8 copy-done.10
  263.3 0.0 copy-start.26
  263.3 0.6 fusion.16
  264.0 2.9 convolution_bitcast_fusion.3
  266.9 2.8 convolution_bitcast_fusion.2
  269.7 1.4 fusion.54
  271.2 156.0 %reduce-scatter.2.cloned.1.call-done = f32[6,1,192,128]{3,2,0,1:T(8,128)} async-done(((f32[192,1,192,128]{3,2,0,1:T(8,128)}), f32[6,1,192,128]{3,2,0,1:T(8,128)}) %reduce-scatter.2.cloned.1.call-update) | async-done | bytes 589840 | tf_op jit(solution)/shard_map/reduce_scatter | solution.py:53
  427.2 1.7 fusion.41
  428.9 0.8 copy-done.11
  429.7 0.2 copy-done.12
  429.9 0.2 copy-done.13
  430.1 0.2 copy-done.14
  430.3 2.7 fusion.17
  433.0 4.1 fusion.30
  437.1 75.8 %psum.31 = f32[2,128]{1,0:T(2,128)} all-reduce(f32[2,128]{1,0:T(2,128)S(1)} %pad_maximum_fusion), channel_id=1, replica_groups=mesh['dp'=8,'dap'=32] {'dp','dap'}, use_global_device_ids=true, to_apply=%region_14.0 | all-reduce | flops 256 | bytes 2048 | tf_op jit(solution)/shard_map/psum | solution.py:79
  513.0 0.3 multiply_reduce_fusion.3
  513.3 0.0 all-reduce.3.cloned.1.call-update
  513.3 1.5 fusion.32
  514.8 243.3 %all-reduce.3.cloned.1.call-done = (f32[128,512]{1,0:T(8,128)}, f32[128,128]{1,0:T(8,128)}, f32[128,128]{1,0:T(8,128)}) async-done(((f32[128,512]{1,0:T(8,128)}, f32[128,128]{1,0:T(8,128)}, f32[128,128]{1,0:T(8,128)}), (f32[128,512]{1,0:T(8,128)}, f32[128,128]{1,0:T(8,128)}, f32[128,128]{1,0:T(8,128)})) %all-reduce.3.cloned.1.call-update) | async-done | bytes 393232 | tf_op jit(solution)/shard_map/psum | solution.py:79
  758.1 1.7 copy.35
  759.8 1.5 copy.36
  761.3 1.5 copy.37
  (52 shorter events, 0.1 us)
Async XLA Ops:
  7.2 4.6 copy-start
  7.2 132.5 %all-gather.2.cloned.1.call-start = ((), (), s32[]{:S(2)}) async-start(), calls=%async_computation.1 | async-start | bytes 19464192 | tf_op jit(solution)/shard_map/all_gather | solution.py:37
  8.7 9.1 %copy-start.29 = (f32[128]{0:T(128)}, f32[128]{0:T(128)S(1)}, u32[]{:S(2)}) copy-start(f32[128]{0:T(128)S(1)} %get-tuple-element.22) | copy-start | bytes 1540
  8.7 15.2 %copy-start.27 = (f32[128]{0:T(128)}, f32[128]{0:T(128)S(1)}, u32[]{:S(2)}) copy-start(f32[128]{0:T(128)S(1)} %get-tuple-element.21) | copy-start | bytes 1540
  11.6 6.2 copy-start.19
  11.8 5.8 copy-start.23
  14.9 1.4 copy-start.1
  16.4 1.5 copy-start.3
  16.4 1.5 copy-start.25
  17.6 2.0 copy-start.5
  17.6 2.0 copy-start.16
  17.6 409.6 %reduce-scatter.2.cloned.1.call-start = ((), (), s32[]{:S(2)}) async-start(), calls=%async_computation.2 | async-start | bytes 19464192 | tf_op jit(solution)/shard_map/reduce_scatter | solution.py:53
  18.7 0.8 copy-start.7
  164.5 25.5 %copy-start.28 = (f32[128]{0:T(128)S(1)}, f32[128]{0:T(128)}, u32[]{:S(2)}) copy-start(f32[128]{0:T(128)} %copy-done.27) | copy-start | bytes 1540
  189.7 3.6 copy-start.4
  189.8 3.6 copy-start.21
  190.0 2.8 copy-start.18
  192.8 0.6 copy-start.22
  240.6 517.5 %all-reduce.3.cloned.1.call-start = ((), (), s32[]{:S(2)}) async-start(), calls=%async_computation.3 | async-start | bytes 786432 | tf_op jit(solution)/shard_map/psum | solution.py:79
  258.5 4.8 copy-start.8
  258.5 4.8 copy-start.17
  260.9 3.1 copy-start.20
  262.5 0.8 copy-start.10
  263.3 3.6 copy-start.6
  263.3 3.6 copy-start.9
  263.3 6.4 copy-start.26
  264.0 163.2 %copy-start.2 = (f32[1,6,192,512]{3,2,1,0:T(8,128)S(1)}, f32[1,6,192,512]{3,2,1,0:T(8,128)}, u32[]{:S(2)}) copy-start(f32[1,6,192,512]{3,2,1,0:T(8,128)} %copy-done.1) | copy-start | bytes 7077892
  264.0 163.2 %copy-start.24 = (f32[6,192]{1,0:T(8,128)S(1)}, f32[6,192]{1,0:T(8,128)}, u32[]{:S(2)}) copy-start(f32[6,192]{1,0:T(8,128)} %copy-done.23) | copy-start | bytes 13828
  271.2 159.1 %copy-start.30 = (f32[128]{0:T(128)S(1)}, f32[128]{0:T(128)}, u32[]{:S(2)}) copy-start(f32[128]{0:T(128)} %copy-done.29) | copy-start | bytes 1540
  428.9 0.8 copy-start.11
  428.9 1.0 copy-start.12
  428.9 1.2 copy-start.13
  428.9 1.4 copy-start.14
  430.3 2.7 copy-start.15
  433.0 4.1 copy-start.31
Sparse Core Ops, SparseCore 0:
  17.7 121.9 all-gather.1
  240.7 186.3 reduce-scatter.1
  513.4 244.6 all-reduce.2
where the time goes:
time: 771 us; the launch traced here: 769 us
  waiting for transfers between devices  514 us (67%)
  matrix products  87.1 us (11%)
  blocking collectives  75.8 us (10%)
  local copies, waits for them, and re-layouts  65.5 us (8%)
  between operations  14.1 us (2%)
  other arithmetic  12.1 us (2%)
    psum x1, waiting for transfers between devices, shards(): lax.psum((grad_w_in, grad_w_gate, grad_w_out, grad_gains), ('dp', 'dap'))  243 us
    reduce_scatter x1, waiting for transfers between devices, shards(): lax.psum_scatter(jnp.einsum('sijh,sikh->jskh', triangle_gradient, a_val,...  156 us
    all_gather x1, waiting for transfers between devices, shards(): b_whole = lax.all_gather(b_val, 'dap', axis=1, tiled=True)  115 us
    psum x1, blocking collectives, shards(): lax.psum((grad_w_in, grad_w_gate, grad_w_out, grad_gains), ('dp', 'dap'))  75.8 us
    dot_general x1, matrix products, shards(): jnp.einsum('sikh,sjkh->sijh', a_val, b_whole, precision=HIGH)  25.2 us
    all_gather x1, local copies, waits for them, and re-layouts, shards(): b_whole = lax.all_gather(b_val, 'dap', axis=1, tiled=True)  24.8 us
    dot_general x1, matrix products, shards(): jnp.einsum('sijh,sikh->jskh', triangle_gradient, a_val, precision=HIGH)  24 us
    dot_general x1, local copies, waits for them, and re-layouts, shards(): jnp.einsum('sijh,sikh->jskh', triangle_gradient, a_val, precision=HIGH)  23.2 us
  transfers between devices with their start and end apart: 3, of which 3 were waited for; matrix products, arithmetic and copies ran while one was open for 5% of the time, Pallas kernels for 0%

commit v1 on v0

v1 whole, which is shorter than its diff:
```python
import functools

import jax
import jax.numpy as jnp
from jax import lax
from jax.experimental import pallas as pl
from jax.experimental.pallas import tpu as pltpu
from jax.sharding import PartitionSpec as P

F32 = jnp.float32
BF16 = jnp.bfloat16
LANES = 384
EPS = 1e-05


def parts(x):
    hi = x.astype(BF16)
    return hi, (x - hi.astype(F32)).astype(BF16)


def dot3(left, right, dims=((1,), (0,))):
    (ah, al), (bh, bl) = left, right

    def one(a, b):
        return lax.dot_general(a, b, (dims, ((), ())), preferred_element_type=F32)

    return one(ah, bh) + (one(ah, bl) + one(al, bh))


NT = ((1,), (1,))
TN = ((0,), (0,))


def column(row):
    n = row.shape[1]
    return jnp.broadcast_to(row, (n, n)).T[:, :1]


def hat(x):
    center = x - jnp.mean(x, axis=0, keepdims=True)
    inverse = lax.rsqrt(jnp.mean(center * center, axis=0, keepdims=True) + EPS)
    return center * inverse, inverse


def hat_back(g, xhat, inverse):
    first = jnp.mean(g, axis=0, keepdims=True)
    second = jnp.mean(g * xhat, axis=0, keepdims=True)
    return inverse * (g - first - xhat * second)


def call(body, outs, scratch=(), flops=0, moved=0):
    return pl.pallas_call(
        body,
        out_shape=[jax.ShapeDtypeStruct(s, d) for s, d in outs],
        scratch_shapes=list(scratch),
        compiler_params=pltpu.CompilerParams(vmem_limit_bytes=40 * 2**20),
        cost_estimate=pl.CostEstimate(flops=flops, bytes_accessed=moved, transcendentals=0),
    )


def cell_slices(c, res):
    base = pl.multiple_of(c * 2 * res, 2 * res)
    return (
        pl.ds(base, 128),
        pl.ds(base + 128, res - 128),
        pl.ds(base + res + 128, res - 128),
        pl.ds(base + res, 128),
    )


def load_cells(ref, c, res):
    return jnp.concatenate([ref[at, :] for at in cell_slices(c, res)], axis=0).T


def store_cells(ref, c, res, value):
    value = value.T
    start = 0
    for at in cell_slices(c, res):
        ref[at, :] = value[start : start + at.size, :]
        start += at.size


def tile_rows(n, kinds, tile, kind):
    return pl.ds(tile * kinds + kind, n, stride=9 * kinds)


def to_rows(tiles):
    return (tiles[0], tiles[1]), (tiles[2], pltpu.roll(tiles[1], 64, 1))


def to_tiles(even, odd):
    low = lax.broadcasted_iota(jnp.int32, even[1].shape, 1) < 64
    return even[0], jnp.where(low, even[1], pltpu.roll(odd[1], 64, 1)), odd[0]


def project_kernel(n, res, pair, w_in, gains, send, zhat, zinv, val, sig, wt_hi, wt_lo):
    hidden = w_in.shape[1] // 4
    per = hidden // n
    wh, wl = parts(w_in[...].T)
    wt_hi[...], wt_lo[...] = wh, wl
    gain = column(gains[0:1, :])

    def step(c, _):
        at = pl.ds(pl.multiple_of(c * LANES, LANES), LANES)
        z, inverse = hat(load_cells(pair, c, res))
        zhat[:, at] = z
        zinv[:, at] = inverse
        zn = parts(z * gain)
        for which in range(2):
            rows = pl.ds(2 * which * hidden, hidden)
            gate_rows = pl.ds((2 * which + 1) * hidden, hidden)
            value = dot3((wt_hi[rows, :], wt_lo[rows, :]), zn)
            gate = jax.nn.sigmoid(dot3((wt_hi[gate_rows, :], wt_lo[gate_rows, :]), zn))
            val[pl.ds(which * hidden, hidden), at] = value
            sig[pl.ds(which * hidden, hidden), at] = gate
            both = value * gate
            for q in range(per):
                for t in range(3):
                    send[tile_rows(n, 2 * per, 3 * c + t, which * per + q), :] = both[
                        q * n : (q + 1) * n, t * 128 : (t + 1) * 128
                    ]
        return 0

    lax.fori_loop(0, pair.shape[0] // LANES, step, 0)


def make_masks(mask, line, swap, rows):
    res = mask.shape[1]
    line[...] = jnp.zeros_like(line)
    line[0:1, pl.ds(0, res)] = mask[...].astype(F32)
    across = jnp.broadcast_to(line[0:1, :], (256, 256))
    both = across * across.T
    swap[0:256, :] = both[:, :128]
    swap[256:512, :] = both[:, 128:]
    n = res // rows
    return [[swap[pl.ds(256 * half + il, n, stride=rows), :] for half in range(2)] for il in range(rows)]


MASK_SCRATCH = [pltpu.VMEM((8, 256), F32), pltpu.VMEM((512, 128), F32)]


def triangle_kernel(n, got, mask, send, a_out, b_out, line, swap):
    per = got.shape[0] // (2 * 9 * n)
    res = mask.shape[1]
    rows = res // n
    pm = make_masks(mask, line, swap, rows)
    for q in range(per):
        base = 512 * q
        for half in range(2):
            b_out[pl.ds(base + 256 * half + res, 256 - res), :] = jnp.zeros((256 - res, 128), F32)
        for p in range(rows // 2):
            two_a = to_rows([got[tile_rows(n, 2 * per, 3 * p + t, q), :] for t in range(3)])
            two_b = to_rows([got[tile_rows(n, 2 * per, 3 * p + t, per + q), :] for t in range(3)])
            for side in range(2):
                il = 2 * p + side
                for half in range(2):
                    a_out[q, pl.ds(il * n, n), pl.ds(128 * half, 128)] = two_a[side][half] * pm[il][half]
                    b_out[pl.ds(base + 256 * half + il, n, stride=rows), :] = two_b[side][half] * pm[il][half]
        b_whole = jnp.concatenate([b_out[pl.ds(base, 256), :], b_out[pl.ds(base + 256, 256), :]], axis=1)
        x = dot3(parts(a_out[q]), parts(b_whole), NT)
        for p in range(rows // 2):
            even, odd = [
                [x[(2 * p + side) * n : (2 * p + side + 1) * n, 128 * half : 128 * half + 128] for half in range(2)]
                for side in range(2)
            ]
            for t, tile in enumerate(to_tiles(even, odd)):
                send[tile_rows(n, per, 3 * p + t, q), :] = tile


def output_kernel(n, res, got, up, zhat, w_gate, w_out, gains, send, dzn, mg, mo, wgt, wot):
    hidden = w_out.shape[0]
    per = hidden // n
    gain0, gain1 = column(gains[0:1, :]), column(gains[1:2, :])
    wgt[...] = w_gate[...].T
    wot[...] = w_out[...].T
    mg[...] = jnp.zeros_like(mg)
    mo[...] = jnp.zeros_like(mo)

    def step(c, _):
        at = pl.ds(pl.multiple_of(c * LANES, LANES), LANES)
        x = jnp.concatenate(
            [
                jnp.concatenate([got[tile_rows(n, per, 3 * c + t, q), :] for q in range(per)], axis=0)
                for t in range(3)
            ],
            axis=1,
        )
        xhat, inverse = hat(x)
        z = zhat[:, at]
        z_parts = parts(z)
        upstream = load_cells(up, c, res)
        gate = jax.nn.sigmoid(dot3(parts(wgt[...]), parts(z * gain0)))
        out = dot3(parts(wot[...]), parts(xhat * gain1))
        d_out = parts(upstream * gate)
        d_logit = parts(upstream * out * gate * (1.0 - gate))
        mo[...] += dot3(d_out, parts(xhat), NT)
        mg[...] += dot3(d_logit, z_parts, NT)
        dzn[:, at] = dot3(parts(w_gate[...]), d_logit)
        g = dot3(parts(w_out[...]), d_out) * gain1
        dx = hat_back(g, xhat, inverse)
        for q in range(per):
            for t in range(3):
                send[tile_rows(n, per, 3 * c + t, q), :] = dx[q * n : (q + 1) * n, t * 128 : (t + 1) * 128]
        return 0

    lax.fori_loop(0, up.shape[0] // LANES, step, 0)


def triangle_back_kernel(n, got, mask, a_in, b_in, send, line, swap, dx_all, db_all):
    per = got.shape[0] // (9 * n)
    res = mask.shape[1]
    rows = res // n
    pm = make_masks(mask, line, swap, rows)
    for q in range(per):
        base = 512 * q
        for p in range(rows // 2):
            two = to_rows([got[tile_rows(n, per, 3 * p + t, q), :] for t in range(3)])
            for side in range(2):
                for half in range(2):
                    dx_all[pl.ds((2 * p + side) * n, n), pl.ds(128 * half, 128)] = two[side][half]
        dx = parts(dx_all[...])
        b_whole = jnp.concatenate([b_in[pl.ds(base, 256), :], b_in[pl.ds(base + 256, 256), :]], axis=1)
        da = dot3(dx, parts(b_whole))
        db = dot3(dx, parts(a_in[q]), TN)
        db_all[0:256, :] = db[:, :128]
        db_all[256:512, :] = db[:, 128:]
        for p in range(rows // 2):
            two_a, two_b = [], []
            for il in (2 * p, 2 * p + 1):
                two_a.append([da[il * n : (il + 1) * n, 128 * half : 128 * half + 128] * pm[il][half] for half in range(2)])
                two_b.append([db_all[pl.ds(256 * half + il, n, stride=rows), :] * pm[il][half] for half in range(2)])
            for t, tile in enumerate(to_tiles(*two_a)):
                send[tile_rows(n, 2 * per, 3 * p + t, q), :] = tile
            for t, tile in enumerate(to_tiles(*two_b)):
                send[tile_rows(n, 2 * per, 3 * p + t, per + q), :] = tile


def input_kernel(n, res, got, zhat, zinv, val, sig, dzn, w_in, gains, d_pair, mi, w_hi, w_lo):
    hidden = w_in.shape[1] // 4
    per = hidden // n
    wh, wl = parts(w_in[...])
    w_hi[...], w_lo[...] = wh, wl
    gain0 = column(gains[0:1, :])
    mi[...] = jnp.zeros_like(mi)

    def step(c, _):
        at = pl.ds(pl.multiple_of(c * LANES, LANES), LANES)
        z = zhat[:, at]
        z_parts = parts(z)
        total = dzn[:, at]
        for which in range(2):
            d = jnp.concatenate(
                [
                    jnp.concatenate(
                        [got[tile_rows(n, 2 * per, 3 * c + t, which * per + q), :] for q in range(per)], axis=0
                    )
                    for t in range(3)
                ],
                axis=1,
            )
            rows = pl.ds(which * hidden, hidden)
            gate = sig[rows, at]
            d_val = d * gate
            d_gate = d_val * val[rows, at] * (1.0 - gate)
            for k, grad in ((2 * which, d_val), (2 * which + 1, d_gate)):
                cols = pl.ds(k * hidden, hidden)
                grad = parts(grad)
                total += dot3((w_hi[:, cols], w_lo[:, cols]), grad)
                mi[cols, :] += dot3(grad, z_parts, NT)
        store_cells(d_pair, c, res, hat_back(total * gain0, z, zinv[:, at]))
        return 0

    lax.fori_loop(0, d_pair.shape[0] // LANES, step, 0)


def finish_kernel(m, w_in, w_gate, w_out, gains, d_w_in, d_w_gate, d_w_out, d_gains):
    width = w_out.shape[0]
    gain0, gain1 = column(gains[0:1, :]), column(gains[1:2, :])
    fold = jnp.zeros((width, width), F32)
    for k in range(w_in.shape[1] // width):
        cols = pl.ds(k * width, width)
        part = m[cols, :].T
        d_w_in[:, cols] = part * gain0
        fold += part * w_in[:, cols]
    base = w_in.shape[1]
    part = m[pl.ds(base, width), :].T
    d_w_gate[...] = part * gain0
    fold += part * w_gate[...]
    d_gains[0:1, :] = jnp.sum(fold.T, axis=0, keepdims=True)
    part = m[pl.ds(base + width, width), :].T
    d_w_out[...] = part * gain1
    d_gains[1:2, :] = jnp.sum((part * w_out[...]).T, axis=0, keepdims=True)


def exchange(x, axis):
    return lax.all_to_all(x, axis, 0, 0, tiled=True)


def shards(n, n_dp, pair, upstream, residue_mask, w_in, w_gate, w_out, gains):
    _, rows, res, width = pair.shape
    hidden = w_out.shape[0]
    cells = rows * res
    per = hidden // n
    pair2 = pair.reshape(cells, width)
    up2 = upstream.reshape(cells, width)
    tiles = n * 9 * per

    def wide(x):
        return exchange(x.reshape(n, 18 * per, 128), "dap").reshape(2 * tiles, 128)

    def narrow(x):
        return exchange(x.reshape(n * 9, per, 128), "dap").reshape(tiles, 128)

    send, zhat, zinv, val, sig = call(
        functools.partial(project_kernel, n, res),
        [
            ((2 * tiles, 128), F32),
            ((width, cells), F32),
            ((1, cells), F32),
            ((2 * hidden, cells), F32),
            ((2 * hidden, cells), F32),
        ],
        [pltpu.VMEM((4 * hidden, width), BF16)] * 2,
    )(pair2, w_in, gains)
    got = wide(send)

    send, a_all, b_all = call(
        functools.partial(triangle_kernel, n),
        [((tiles, 128), F32), ((per, res, 256), F32), ((per * 512, 128), F32)],
        MASK_SCRATCH,
    )(got, residue_mask)
    got = narrow(send)

    send, dzn, mg, mo = call(
        functools.partial(output_kernel, n, res),
        [
            ((tiles, 128), F32),
            ((width, cells), F32),
            ((width, width), F32),
            ((width, hidden), F32),
        ],
        [pltpu.VMEM((width, width), F32), pltpu.VMEM((width, hidden), F32)],
    )(got, up2, zhat, w_gate, w_out, gains)
    got = narrow(send)

    (send,) = call(
        functools.partial(triangle_back_kernel, n),
        [((2 * tiles, 128), F32)],
        MASK_SCRATCH + [pltpu.VMEM((res, 256), F32), pltpu.VMEM((512, 128), F32)],
    )(got, residue_mask, a_all, b_all)
    got = wide(send)

    d_pair, mi = call(
        functools.partial(input_kernel, n, res),
        [((cells, width), F32), ((4 * hidden, width), F32)],
        [pltpu.VMEM((width, 4 * hidden), BF16)] * 2,
    )(got, zhat, zinv, val, sig, dzn, w_in, gains)

    m = jnp.concatenate([mi, mg, mo], axis=0)
    count = m.shape[0]
    mine = jnp.sum(exchange(m.reshape(n, count // n, width), "dap"), axis=0)
    mine = jnp.broadcast_to(mine[None], (n_dp,) + mine.shape)
    mine = jnp.sum(exchange(mine, "dp"), axis=0)
    m = exchange(jnp.broadcast_to(mine[None], (n,) + mine.shape), "dap").reshape(count, width)

    d_w_in, d_w_gate, d_w_out, d_gains = call(
        finish_kernel,
        [(w_in.shape, F32), (w_gate.shape, F32), (w_out.shape, F32), (gains.shape, F32)],
    )(m, w_in, w_gate, w_out, gains)
    return (d_pair.reshape(pair.shape), d_w_in, d_w_gate, d_w_out, d_gains)


def solution(mesh):
    cells = P("dp", "dap", None, None)
    in_specs = (cells, cells, P("dp", None), P(), P(), P(), P())
    out_specs = (cells, P(), P(), P(), P())
    body = functools.partial(shards, mesh.shape["dap"], mesh.shape["dp"])
    return jax.shard_map(body, mesh=mesh, in_specs=in_specs, out_specs=out_specs, check_vma=False)
```

time: 771 us -> 197 us (0.26)
  waiting for transfers between devices: 514 us -> 0 us
  blocking collectives: 75.8 us -> 181 us
  matrix products: 87.1 us -> 0 us
  local copies, waits for them, and re-layouts: 65.5 us -> 2.75 us
  between operations: 14.1 us -> 0.71 us
  Pallas kernels: 0 us -> 12.3 us
  other arithmetic: 12.1 us -> 0.08 us
    psum x1 -> x0, waiting for transfers between devices: 243 us -> none  [shards(): lax.psum((grad_w_in, grad_w_gate, grad_w_out, grad_gains), ('dp', 'dap'))]
    all_to_all x0 -> x7, blocking collectives: none -> 181 us  [exchange(): return lax.all_to_all(x, axis, 0, 0, tiled=True)]
    reduce_scatter x1 -> x0, waiting for transfers between devices: 156 us -> none  [shards(): lax.psum_scatter(jnp.einsum('sijh,sikh->jskh', triangle_gradient, a_val,...]
    all_gather x1 -> x0, waiting for transfers between devices: 115 us -> none  [shards(): b_whole = lax.all_gather(b_val, 'dap', axis=1, tiled=True)]
    dot_general x12 -> x0, matrix products: 87.1 us -> none  [the longest x1 25.2 us: shards(): jnp.einsum('sikh,sjkh->sijh', a_val, b_whole, precision=HIGH)]
    psum x1 -> x0, blocking collectives: 75.8 us -> none  [shards(): lax.psum((grad_w_in, grad_w_gate, grad_w_out, grad_gains), ('dp', 'dap'))]
    dot_general x3 -> x0, local copies, waits for them, and re-layouts: 27.2 us -> none  [the longest x1 23.2 us: shards(): jnp.einsum('sijh,sikh->jskh', triangle_gradient, a_val, precision=HIGH)]
    all_gather x1 -> x0, local copies, waits for them, and re-layouts: 24.8 us -> none  [shards(): b_whole = lax.all_gather(b_val, 'dap', axis=1, tiled=True)]
  transfers between devices with their start and end apart: 3 -> 0, of which waited for: 3 -> 0; matrix products, arithmetic and copies ran while one was open for 5% -> 0% of each run, Pallas kernels for 0% -> 0%
where the time goes in v1:
time: 197 us
  blocking collectives  181 us (92%)
  Pallas kernels  12.3 us (6%)
  local copies, waits for them, and re-layouts  2.75 us (1%)
    all_to_all x7, blocking collectives, exchange(): return lax.all_to_all(x, axis, 0, 0, tiled=True)  181 us
    pallas_call x1, Pallas kernels, shards(): call(functools.partial(input_kernel, n, res), [((cells, width), F32), ((4...  4.09 us

profile of v1, /device:TPU:1, one launch (start us, length us, event | category | flops | bytes accessed | tf_op | source)
XLA Modules:
  0.0 196.7 jit_solution(13823761691876418847)
XLA Ops:
  0.6 0.0 copy-start
  0.6 0.9 copy-done
  1.6 0.0 copy-start.3
  1.6 1.1 copy-done.3
  2.6 0.0 copy-start.6
  2.7 0.7 copy-done.6
  3.3 2.2 %shard_map.110 = (f32[2304,128]{1,0:T(8,128)S(1)}, f32[128,1152]{1,0:T(8,128)S(1)}, f32[1,1152]{1,0:T(1,128)S(1)}, f32[256,1152]{1,0:T(8,128)S(1)}, f32[256,1152]{1,0:T(8,128)S(1)}) custom-call(f32[1152,128]{1,0:T(8,128)S(1)} %bitcast.21, f32[128,512]{1,0:T(8,128)S(1)} %copy-done, f32[2,128]{1,0:T(2,128)S(1)} %copy-done.6), custom_call_target="tpu_custom_call" | custom-call | tf_op jit(solution)/shard_map/pallas_call | solution.py:314
  5.5 0.0 copy-start.8
  5.5 46.0 %all_to_all.35 = f32[32,72,128]{2,1,0:T(8,128)S(1)} all-to-all(f32[32,72,128]{2,1,0:T(8,128)S(1)} %bitcast.19), channel_id=1, replica_groups=mesh['dp'=8,'dap'=32] {'dap'}, dimensions={0} | all-to-all | bytes 2359296 | tf_op jit(solution)/shard_map/all_to_all | solution.py:296
  51.5 0.0 copy-done.8
  51.5 0.0 copy-start.2
  51.5 0.0 copy-start.4
  51.5 0.0 copy-start.5
  51.5 1.0 shard_map.111
  52.5 22.9 %all_to_all.36 = f32[288,4,128]{2,1,0:T(4,128)S(1)} all-to-all(f32[288,4,128]{2,1,0:T(4,128)S(1)} %bitcast.23), channel_id=1, replica_groups=mesh['dp'=8,'dap'=32] {'dap'}, dimensions={0} | all-to-all | bytes 1179648 | tf_op jit(solution)/shard_map/all_to_all | solution.py:296
  75.5 0.0 copy-done.2
  75.5 0.0 copy-done.4
  75.5 0.0 copy-done.5
  75.5 2.9 %shard_map.112 = (f32[1152,128]{1,0:T(8,128)S(1)}, f32[128,1152]{1,0:T(8,128)S(1)}, f32[128,128]{1,0:T(8,128)S(1)}, f32[128,128]{1,0:T(8,128)S(1)}) custom-call(f32[1152,128]{1,0:T(8,128)S(1)} %bitcast.16, f32[1152,128]{1,0:T(8,128)S(1)} %bitcast.20, f32[128,1152]{1,0:T(8,128)S(1)} %get-tuple-element.25.zhat, f32[128,128]{1,0:T(8,128)S(1)} %copy-done.4, ...), custom_call_target="tpu_custom_call" | custom-call | tf_op jit(solution)/shard_map/pallas_call | solution.py:334
  78.3 24.2 %all_to_all.37 = f32[288,4,128]{2,1,0:T(4,128)S(1)} all-to-all(f32[288,4,128]{2,1,0:T(4,128)S(1)} %bitcast.22), channel_id=1, replica_groups=mesh['dp'=8,'dap'=32] {'dap'}, dimensions={0} | all-to-all | bytes 1179648 | tf_op jit(solution)/shard_map/all_to_all | solution.py:296
  102.6 1.2 shard_map.113
  103.8 0.0 copy-start.1
  103.8 0.0 copy-start.7
  103.8 37.4 %all_to_all.38 = f32[32,72,128]{2,1,0:T(8,128)S(1)} all-to-all(f32[32,72,128]{2,1,0:T(8,128)S(1)} %bitcast.15), channel_id=1, replica_groups=mesh['dp'=8,'dap'=32] {'dap'}, dimensions={0} | all-to-all | bytes 2359296 | tf_op jit(solution)/shard_map/all_to_all | solution.py:296
  141.2 0.0 copy-done.1
  141.2 0.0 copy-done.7
  141.2 4.1 %shard_map.114 = (f32[1152,128]{1,0:T(8,128)}, f32[512,128]{1,0:T(8,128)S(1)}) custom-call(f32[2304,128]{1,0:T(8,128)S(1)} %bitcast.13, f32[128,1152]{1,0:T(8,128)S(1)} %get-tuple-element.25.zhat, f32[1,1152]{1,0:T(1,128)S(1)} %get-tuple-element.29.zinv, f32[256,1152]{1,0:T(8,128)S(1)} %get-tuple-element.30.val, f32[256,1152]{1,0:T(8,128)S(1)} %get-tuple-element.31.sig, ...), custom_call_target="tpu_custom_call" | custom-call | tf_op jit(solution)/shard_map/pallas_call | solution.py:353
  145.4 19.8 %all_to_all.39 = f32[32,24,128]{2,1,0:T(8,128)S(1)} all-to-all(f32[32,24,128]{2,1,0:T(8,128)S(1)} %bitcast.24), channel_id=1, replica_groups=mesh['dp'=8,'dap'=32] {'dap'}, dimensions={0} | all-to-all | bytes 786432 | tf_op jit(solution)/shard_map/all_to_all | solution.py:296
  165.2 9.1 %all_to_all.40 = f32[8,24,128]{2,1,0:T(8,128)S(1)} all-to-all(f32[8,24,128]{2,1,0:T(8,128)S(1)} %broadcast_in_dim.4), channel_id=1, replica_groups=mesh['dp'=8,'dap'=32] {'dp'}, dimensions={0} | all-to-all | bytes 196608 | tf_op jit(solution)/shard_map/all_to_all | solution.py:296
  174.4 21.4 %all_to_all.41 = f32[32,24,128]{2,1,0:T(8,128)S(1)} all-to-all(f32[32,24,128]{2,1,0:T(8,128)S(1)} %broadcast_in_dim.5), channel_id=1, replica_groups=mesh['dp'=8,'dap'=32] {'dap'}, dimensions={0} | all-to-all | bytes 786432 | tf_op jit(solution)/shard_map/all_to_all | solution.py:296
  195.7 1.0 shard_map.115
  (5 shorter events, 0.1 us)
Async XLA Ops:
  0.6 1.0 copy-start
  1.6 1.1 copy-start.3
  2.6 0.7 copy-start.6
  5.5 46.0 %copy-start.8 = (s32[1,192]{1,0:T(1,128)S(1)}, s32[1,192]{1,0:T(1,128)}, u32[]{:S(2)}) copy-start(s32[1,192]{1,0:T(1,128)} %mask.3) | copy-start | bytes 2308
  51.5 24.0 %copy-start.2 = (f32[1,6,192,128]{3,2,1,0:T(8,128)S(1)}, f32[1,6,192,128]{3,2,1,0:T(8,128)}, u32[]{:S(2)}) copy-start(f32[1,6,192,128]{3,2,1,0:T(8,128)} %param.8) | copy-start | bytes 1769476
  51.5 24.0 %copy-start.4 = (f32[128,128]{1,0:T(8,128)S(1)}, f32[128,128]{1,0:T(8,128)}, u32[]{:S(2)}) copy-start(f32[128,128]{1,0:T(8,128)} %w_gate.3) | copy-start | bytes 196612
  51.5 24.0 %copy-start.5 = (f32[128,128]{1,0:T(8,128)S(1)}, f32[128,128]{1,0:T(8,128)}, u32[]{:S(2)}) copy-start(f32[128,128]{1,0:T(8,128)} %w_out.3) | copy-start | bytes 196612
  103.8 37.5 %copy-start.1 = (f32[128,512]{1,0:T(8,128)S(1)}, f32[128,512]{1,0:T(8,128)}, u32[]{:S(2)}) copy-start(f32[128,512]{1,0:T(8,128)} %w_in.5) | copy-start | bytes 786436
  103.8 37.5 %copy-start.7 = (f32[2,128]{1,0:T(2,128)S(1)}, f32[2,128]{1,0:T(2,128)}, u32[]{:S(2)}) copy-start(f32[2,128]{1,0:T(2,128)} %gains.7) | copy-start | bytes 3076

commit v2 on v1

--- a/solution.py
+++ b/solution.py
@@ -124,7 +124,7 @@
     lax.fori_loop(0, pair.shape[0] // LANES, step, 0)
 
 
-def make_masks(mask, line, swap, rows):
+def make_masks(mask, line, swap, n):
     res = mask.shape[1]
     line[...] = jnp.zeros_like(line)
     line[0:1, pl.ds(0, res)] = mask[...].astype(F32)
@@ -132,30 +132,47 @@
     both = across * across.T
     swap[0:256, :] = both[:, :128]
     swap[256:512, :] = both[:, 128:]
-    n = res // rows
+    rows = res // n
     return [[swap[pl.ds(256 * half + il, n, stride=rows), :] for half in range(2)] for il in range(rows)]
 
 
 MASK_SCRATCH = [pltpu.VMEM((8, 256), F32), pltpu.VMEM((512, 128), F32)]
 
 
-def triangle_kernel(n, got, mask, send, a_out, b_out, line, swap):
+def core_of():
+    return lax.rem(lax.axis_index("dap"), 2)
+
+
+def by_core(mine, other):
+    first = core_of() == 0
+    return jnp.where(first, mine, other), jnp.where(first, other, mine)
+
+
+def triangle_kernel(n, got, other, mask, send, a_out, b_out, line, swap):
     per = got.shape[0] // (2 * 9 * n)
     res = mask.shape[1]
-    rows = res // n
-    pm = make_masks(mask, line, swap, rows)
+    rows = res // (2 * n)
+    pm = make_masks(mask, line, swap, n)
     for q in range(per):
         base = 512 * q
         for half in range(2):
             b_out[pl.ds(base + 256 * half + res, 256 - res), :] = jnp.zeros((256 - res, 128), F32)
         for p in range(rows // 2):
             two_a = to_rows([got[tile_rows(n, 2 * per, 3 * p + t, q), :] for t in range(3)])
-            two_b = to_rows([got[tile_rows(n, 2 * per, 3 * p + t, per + q), :] for t in range(3)])
+            mine = [got[tile_rows(n, 2 * per, 3 * p + t, per + q), :] for t in range(3)]
+            theirs = [other[tile_rows(n, per, 3 * p + t, q), :] for t in range(3)]
+            tiles = [by_core(m, o) for m, o in zip(mine, theirs)]
+            two_b = [to_rows([tile[core] for tile in tiles]) for core in range(2)]
             for side in range(2):
                 il = 2 * p + side
                 for half in range(2):
-                    a_out[q, pl.ds(il * n, n), pl.ds(128 * half, 128)] = two_a[side][half] * pm[il][half]
-                    b_out[pl.ds(base + 256 * half + il, n, stride=rows), :] = two_b[side][half] * pm[il][half]
+                    own = by_core(*[pm[core * rows + il][half] for core in range(2)])[0]
+                    a_out[q, pl.ds(il * n, n), pl.ds(128 * half, 128)] = two_a[side][half] * own
+                    for core in range(2):
+                        row = core * rows + il
+                        b_out[pl.ds(base + 256 * half + row, n, stride=2 * rows), :] = (
+                            two_b[core][side][half] * pm[row][half]
+                        )
         b_whole = jnp.concatenate([b_out[pl.ds(base, 256), :], b_out[pl.ds(base + 256, 256), :]], axis=1)
         x = dot3(parts(a_out[q]), parts(b_whole), NT)
         for p in range(rows // 2):
@@ -206,36 +223,60 @@
     lax.fori_loop(0, up.shape[0] // LANES, step, 0)
 
 
-def triangle_back_kernel(n, got, mask, a_in, b_in, send, line, swap, dx_all, db_all):
+def gather_dx(n, got, q, dx_all):
+    per = got.shape[0] // (9 * n)
+    for p in range(3):
+        two = to_rows([got[tile_rows(n, per, 3 * p + t, q), :] for t in range(3)])
+        for side in range(2):
+            for half in range(2):
+                dx_all[pl.ds((2 * p + side) * n, n), pl.ds(128 * half, 128)] = two[side][half]
+    return parts(dx_all[...])
+
+
+def b_back_kernel(n, got, mask, a_in, keep, give, line, swap, dx_all, db_all):
     per = got.shape[0] // (9 * n)
     res = mask.shape[1]
-    rows = res // n
-    pm = make_masks(mask, line, swap, rows)
+    rows = res // (2 * n)
+    pm = make_masks(mask, line, swap, n)
     for q in range(per):
-        base = 512 * q
-        for p in range(rows // 2):
-            two = to_rows([got[tile_rows(n, per, 3 * p + t, q), :] for t in range(3)])
-            for side in range(2):
-                for half in range(2):
-                    dx_all[pl.ds((2 * p + side) * n, n), pl.ds(128 * half, 128)] = two[side][half]
-        dx = parts(dx_all[...])
-        b_whole = jnp.concatenate([b_in[pl.ds(base, 256), :], b_in[pl.ds(base + 256, 256), :]], axis=1)
-        da = dot3(dx, parts(b_whole))
-        db = dot3(dx, parts(a_in[q]), TN)
+        db = dot3(gather_dx(n, got, q, dx_all), parts(a_in[q]), TN)
         db_all[0:256, :] = db[:, :128]
         db_all[256:512, :] = db[:, 128:]
         for p in range(rows // 2):
-            two_a, two_b = [], []
+            tiles = []
+            for core in range(2):
+                two = []
+                for row in (core * rows + 2 * p, core * rows + 2 * p + 1):
+                    two.append(
+                        [db_all[pl.ds(256 * half + row, n, stride=2 * rows), :] * pm[row][half] for half in range(2)]
+                    )
+                tiles.append(to_tiles(*two))
+            for t in range(3):
+                at = tile_rows(n, per, 3 * p + t, q)
+                keep[at, :], give[at, :] = by_core(tiles[0][t], tiles[1][t])
+
+
+def a_back_kernel(n, got, mask, b_in, keep, taken, send, line, swap, dx_all):
+    per = got.shape[0] // (9 * n)
+    res = mask.shape[1]
+    rows = res // (2 * n)
+    pm = make_masks(mask, line, swap, n)
+    for q in range(per):
+        base = 512 * q
+        b_whole = jnp.concatenate([b_in[pl.ds(base, 256), :], b_in[pl.ds(base + 256, 256), :]], axis=1)
+        da = dot3(gather_dx(n, got, q, dx_all), parts(b_whole))
+        for p in range(rows // 2):
+            two = []
             for il in (2 * p, 2 * p + 1):
-                two_a.append([da[il * n : (il + 1) * n, 128 * half : 128 * half + 128] * pm[il][half] for half in range(2)])
-                two_b.append([db_all[pl.ds(256 * half + il, n, stride=rows), :] * pm[il][half] for half in range(2)])
-            for t, tile in enumerate(to_tiles(*two_a)):
+                own = [by_core(pm[il][half], pm[rows + il][half])[0] for half in range(2)]
+                two.append([da[il * n : (il + 1) * n, 128 * half : 128 * half + 128] * own[half] for half in range(2)])
+            for t, tile in enumerate(to_tiles(*two)):
+                at = tile_rows(n, per, 3 * p + t, q)
                 send[tile_rows(n, 2 * per, 3 * p + t, q), :] = tile
-            for t, tile in enumerate(to_tiles(*two_b)):
-                send[tile_rows(n, 2 * per, 3 * p + t, per + q), :] = tile
-
-
-def input_kernel(n, res, got, zhat, zinv, val, sig, dzn, w_in, gains, d_pair, mi, w_hi, w_lo):
+                send[tile_rows(n, 2 * per, 3 * p + t, per + q), :] = keep[at, :] + taken[at, :]
+
+
+def input_kernel(n, res, got, zhat, zinv, val, sig, dzn, w_in, gains, mg, mo, d_pair, keep, give, mi, w_hi, w_lo):
     hidden = w_in.shape[1] // 4
     per = hidden // n
     wh, wl = parts(w_in[...])
@@ -271,10 +312,16 @@
         return 0
 
     lax.fori_loop(0, d_pair.shape[0] // LANES, step, 0)
-
-
-def finish_kernel(m, w_in, w_gate, w_out, gains, d_w_in, d_w_gate, d_w_out, d_gains):
+    half = keep.shape[0]
+    low = mi[pl.ds(0, half), :]
+    high = jnp.concatenate([mi[pl.ds(half, mi.shape[0] - half), :], mg[...], mo[...]], axis=0)
+    keep[...], give[...] = by_core(low, high)
+
+
+def finish_kernel(mine, theirs, w_in, w_gate, w_out, gains, d_w_in, d_w_gate, d_w_out, d_gains, m):
     width = w_out.shape[0]
+    half = mine.shape[0]
+    m[0:half, :], m[half:, :] = by_core(mine[...], theirs[...])
     gain0, gain1 = column(gains[0:1, :]), column(gains[1:2, :])
     fold = jnp.zeros((width, width), F32)
     for k in range(w_in.shape[1] // width):
@@ -292,24 +339,73 @@
     d_gains[1:2, :] = jnp.sum((part * w_out[...]).T, axis=0, keepdims=True)
 
 
-def exchange(x, axis):
-    return lax.all_to_all(x, axis, 0, 0, tiled=True)
-
-
-def shards(n, n_dp, pair, upstream, residue_mask, w_in, w_gate, w_out, gains):
+def exchange(x, axis, groups):
+    return lax.all_to_all(x, axis, 0, 0, tiled=True, axis_index_groups=groups)
+
+
+def swap_cores(x, n):
+    return lax.ppermute(x, "dap", [(i, i ^ 1) for i in range(2 * n)])
+
+
+BOTH = ("dp", "dap")
+NY = 4
+
+
+def plane_and_line(n, n_dp):
+    nx = max(1, n_dp // 2)
+    nlo, nhi = n_dp // nx, n // NY
+
+    def index(x, y, hi, lo, core):
+        return (lo * nx + x) * 2 * n + (y * nhi + hi) * 2 + core
+
+    planes = [
+        [index(x, y, hi, lo, core) for x in range(nx) for y in range(NY)]
+        for hi in range(nhi)
+        for lo in range(nlo)
+        for core in range(2)
+    ]
+    lines = [
+        [index(x, y, hi, lo, core) for hi in range(nhi) for lo in range(nlo)]
+        for x in range(nx)
+        for y in range(NY)
+        for core in range(2)
+    ]
+    return planes, lines
+
+
+def reduce_all(keep, give, n, n_dp):
+    planes, lines = plane_and_line(n, n_dp)
+    count, width = keep.shape
+
+    def summed(x, groups, pieces):
+        return jnp.sum(exchange(x.reshape(pieces, -1, width), BOTH, groups), axis=0)
+
+    def spread(x, pieces):
+        return jnp.broadcast_to(x[None], (pieces,) + x.shape)
+
+    in_plane, in_line = len(planes[0]), len(lines[0])
+    mine = summed(keep + swap_cores(give, n), planes, in_plane)
+    mine = summed(spread(mine, in_line), lines, in_line)
+    mine = exchange(spread(mine, in_plane), BOTH, planes).reshape(count, width)
+    return mine, swap_cores(mine, n)
+
+
+def shards(devices, n_dp, pair, upstream, residue_mask, w_in, w_gate, w_out, gains):
     _, rows, res, width = pair.shape
     hidden = w_out.shape[0]
     cells = rows * res
+    n = devices // 2
     per = hidden // n
+    same_core = [list(range(core, devices, 2)) for core in range(2)]
     pair2 = pair.reshape(cells, width)
     up2 = upstream.reshape(cells, width)
     tiles = n * 9 * per
 
     def wide(x):
-        return exchange(x.reshape(n, 18 * per, 128), "dap").reshape(2 * tiles, 128)
+        return exchange(x.reshape(n, 18 * per, 128), "dap", same_core).reshape(2 * tiles, 128)
 
     def narrow(x):
-        return exchange(x.reshape(n * 9, per, 128), "dap").reshape(tiles, 128)
+        return exchange(x.reshape(n, 9 * per, 128), "dap", same_core).reshape(tiles, 128)
 
     send, zhat, zinv, val, sig = call(
         functools.partial(project_kernel, n, res),
@@ -324,11 +420,12 @@
     )(pair2, w_in, gains)
     got = wide(send)
 
+    other = swap_cores(got.reshape(n * 9, 2, per, 128)[:, 1].reshape(tiles, 128), n)
     send, a_all, b_all = call(
         functools.partial(triangle_kernel, n),
-        [((tiles, 128), F32), ((per, res, 256), F32), ((per * 512, 128), F32)],
+        [((tiles, 128), F32), ((per, res // 2, 256), F32), ((per * 512, 128), F32)],
         MASK_SCRATCH,
-    )(got, residue_mask)
+    )(got, other, residue_mask)
     got = narrow(send)
 
     send, dzn, mg, mo = call(
@@ -343,30 +440,32 @@
     )(got, up2, zhat, w_gate, w_out, gains)
     got = narrow(send)
 
+    keep, give = call(
+        functools.partial(b_back_kernel, n),
+        [((tiles, 128), F32)] * 2,
+        MASK_SCRATCH + [pltpu.VMEM((res // 2, 256), F32), pltpu.VMEM((512, 128), F32)],
+    )(got, residue_mask, a_all)
+    taken = swap_cores(give, n)
     (send,) = call(
-        functools.partial(triangle_back_kernel, n),
+        functools.partial(a_back_kernel, n),
         [((2 * tiles, 128), F32)],
-        MASK_SCRATCH + [pltpu.VMEM((res, 256), F32), pltpu.VMEM((512, 128), F32)],
-    )(got, residue_mask, a_all, b_all)
+        MASK_SCRATCH + [pltpu.VMEM((res // 2, 256), F32)],
+    )(got, residue_mask, b_all, keep, taken)
     got = wide(send)
 
-    d_pair, mi = call(
+    half = (4 * hidden + 2 * width) // 2
+    d_pair, keep, give = call(
         functools.partial(input_kernel, n, res),
-        [((cells, width), F32), ((4 * hidden, width), F32)],
-        [pltpu.VMEM((width, 4 * hidden), BF16)] * 2,
-    )(got, zhat, zinv, val, sig, dzn, w_in, gains)
-
-    m = jnp.concatenate([mi, mg, mo], axis=0)
-    count = m.shape[0]
-    mine = jnp.sum(exchange(m.reshape(n, count // n, width), "dap"), axis=0)
-    mine = jnp.broadcast_to(mine[None], (n_dp,) + mine.shape)
-    mine = jnp.sum(exchange(mine, "dp"), axis=0)
-    m = exchange(jnp.broadcast_to(mine[None], (n,) + mine.shape), "dap").reshape(count, width)
+        [((cells, width), F32), ((half, width), F32), ((half, width), F32)],
+        [pltpu.VMEM((4 * hidden, width), F32)] + [pltpu.VMEM((width, 4 * hidden), BF16)] * 2,
+    )(got, zhat, zinv, val, sig, dzn, w_in, gains, mg, mo)
+    mine, theirs = reduce_all(keep, give, n, n_dp)
 
     d_w_in, d_w_gate, d_w_out, d_gains = call(
         finish_kernel,
         [(w_in.shape, F32), (w_gate.shape, F32), (w_out.shape, F32), (gains.shape, F32)],
-    )(m, w_in, w_gate, w_out, gains)
+        [pltpu.VMEM((2 * half, width), F32)],
+    )(mine, theirs, w_in, w_gate, w_out, gains)
     return (d_pair.reshape(pair.shape), d_w_in, d_w_gate, d_w_out, d_gains)
 
 

time: 197 us -> 189 us (0.959)
  blocking collectives: 181 us -> 154 us
  starting transfers between devices: 0 us -> 10.6 us
  waiting for transfers between devices: 0 us -> 5.4 us
  Pallas kernels: 12.3 us -> 15.1 us
    all_to_all x7, blocking collectives: 181 us -> 154 us  [exchange(): return lax.all_to_all(x, axis, 0, 0, tiled=True, axis_index_groups=groups)]
    ppermute x0 -> x4, starting transfers between devices: none -> 10.6 us  [swap_cores(): return lax.ppermute(x, 'dap', [(i, i ^ 1) for i in range(2 * n)])]
    ppermute x0 -> x4, waiting for transfers between devices: none -> 5.4 us  [swap_cores(): return lax.ppermute(x, 'dap', [(i, i ^ 1) for i in range(2 * n)])]
    pallas_call x2 -> x3, Pallas kernels: 5.29 us -> 7.1 us  [the longest x1 4.27 us: shards(): call(functools.partial(input_kernel, n, res), [((cells, width), F32), ((h...]
  transfers between devices with their start and end apart: 0 -> 4, of which waited for: 0 -> 4; matrix products, arithmetic and copies ran while one was open for 0% -> 0% of each run, Pallas kernels for 0% -> 0%
where the time goes in v2:
time: 189 us; the launch traced here: 188 us
  blocking collectives  154 us (81%)
  Pallas kernels  15.1 us (8%)
  starting transfers between devices  10.6 us (6%)
  waiting for transfers between devices  5.4 us (3%)
  local copies, waits for them, and re-layouts  2.77 us (1%)
    all_to_all x7, blocking collectives, exchange(): return lax.all_to_all(x, axis, 0, 0, tiled=True, axis_index_groups=groups)  154 us
    ppermute x4, starting transfers between devices, swap_cores(): return lax.ppermute(x, 'dap', [(i, i ^ 1) for i in range(2 * n)])  10.6 us
    ppermute x4, waiting for transfers between devices, swap_cores(): return lax.ppermute(x, 'dap', [(i, i ^ 1) for i in range(2 * n)])  5.4 us
    pallas_call x1, Pallas kernels, shards(): call(functools.partial(input_kernel, n, res), [((cells, width), F32), ((h...  4.27 us
  transfers between devices with their start and end apart: 4, of which 4 were waited for; matrix products, arithmetic and copies ran while one was open for 0% of the time, Pallas kernels for 0%

profile of v2, /device:TPU:1, one launch (start us, length us, event | category | flops | bytes accessed | tf_op | source)
XLA Modules:
  0.0 188.4 jit_solution(1293400885945566356)
XLA Ops:
  0.6 0.0 copy-start
  0.6 0.9 copy-done
  1.6 0.0 copy-start.3
  1.6 1.1 copy-done.3
  2.6 0.0 copy-start.6
  2.7 0.7 copy-done.6
  3.3 2.3 %shard_map.110 = (f32[2304,128]{1,0:T(8,128)S(1)}, f32[128,1152]{1,0:T(8,128)S(1)}, f32[1,1152]{1,0:T(1,128)S(1)}, f32[256,1152]{1,0:T(8,128)S(1)}, f32[256,1152]{1,0:T(8,128)S(1)}) custom-call(f32[1152,128]{1,0:T(8,128)S(1)} %bitcast.27, f32[128,512]{1,0:T(8,128)S(1)} %copy-done, f32[2,128]{1,0:T(2,128)S(1)} %copy-done.6), custom_call_target="tpu_custom_call" | custom-call | tf_op jit(solution)/shard_map/pallas_call | solution.py:410
  5.7 41.7 %all_to_all.35 = f32[16,144,128]{2,1,0:T(8,128)S(1)} all-to-all(f32[16,144,128]{2,1,0:T(8,128)S(1)} %bitcast.23), channel_id=1, replica_groups={{0,2,4,6,8,10,12,14,16,18,20,22,24,26,28,30},{1,3,5,7,9,11,13,15,17,19,..., dimensions={0} | all-to-all | bytes 2359296 | tf_op jit(solution)/shard_map/all_to_all | solution.py:343
  47.4 0.0 copy-start.8
  47.4 4.0 %collective-permute-start = (f32[1152,128]{1,0:T(8,128)S(1)}, f32[1152,128]{1,0:T(8,128)S(1)}, u32[]{:S(2)}, u32[]{:S(2)}) collective-permute-start(f32[1152,128]{1,0:T(8,128)S(1)} %slice_bitcast_fusion), channel_id=1, source_target_pairs={{0,1},{1,0},{2,3},{3,2},{4,5},{5,4},{6,7},{7,6},{8,9},{9,8},{10,11... | collective-permute-start | bytes 1769480 | tf_op jit(solution)/shard_map/ppermute | solution.py:347
  51.5 1.6 collective-permute-done.other
  53.1 0.0 copy-done.8
  53.1 0.0 copy-start.2
  53.1 0.0 copy-start.4
  53.1 0.0 copy-start.5
  53.1 1.7 shard_map.111
  54.8 21.1 %all_to_all.36 = f32[16,72,128]{2,1,0:T(8,128)S(1)} all-to-all(f32[16,72,128]{2,1,0:T(8,128)S(1)} %bitcast.28), channel_id=1, replica_groups={{0,2,4,6,8,10,12,14,16,18,20,22,24,26,28,30},{1,3,5,7,9,11,13,15,17,19,..., dimensions={0} | all-to-all | bytes 1179648 | tf_op jit(solution)/shard_map/all_to_all | solution.py:343
  75.9 0.0 copy-done.2
  75.9 0.0 copy-done.4
  75.9 0.0 copy-done.5
  75.9 2.9 %shard_map.112 = (f32[1152,128]{1,0:T(8,128)S(1)}, f32[128,1152]{1,0:T(8,128)S(1)}, f32[128,128]{1,0:T(8,128)S(1)}, f32[128,128]{1,0:T(8,128)S(1)}) custom-call(f32[1152,128]{1,0:T(8,128)S(1)} %bitcast.22, f32[1152,128]{1,0:T(8,128)S(1)} %bitcast.26, f32[128,1152]{1,0:T(8,128)S(1)} %get-tuple-element.28.zhat, f32[128,128]{1,0:T(8,128)S(1)} %copy-done.4, ...), custom_call_target="tpu_custom_call" | custom-call | tf_op jit(solution)/shard_map/pallas_call | solution.py:431
  78.8 24.6 %all_to_all.37 = f32[16,72,128]{2,1,0:T(8,128)S(1)} all-to-all(f32[16,72,128]{2,1,0:T(8,128)S(1)} %bitcast.29), channel_id=1, replica_groups={{0,2,4,6,8,10,12,14,16,18,20,22,24,26,28,30},{1,3,5,7,9,11,13,15,17,19,..., dimensions={0} | all-to-all | bytes 1179648 | tf_op jit(solution)/shard_map/all_to_all | solution.py:343
  103.4 1.4 shard_map.113
  104.8 0.8 collective-permute-start.1
  105.6 1.6 collective-permute-done.1.taken
  107.2 1.4 shard_map.114
  108.6 0.0 copy-start.1
  108.6 34.1 %all_to_all.38 = f32[16,144,128]{2,1,0:T(8,128)S(1)} all-to-all(f32[16,144,128]{2,1,0:T(8,128)S(1)} %bitcast.21), channel_id=1, replica_groups={{0,2,4,6,8,10,12,14,16,18,20,22,24,26,28,30},{1,3,5,7,9,11,13,15,17,19,..., dimensions={0} | all-to-all | bytes 2359296 | tf_op jit(solution)/shard_map/all_to_all | solution.py:343
  142.7 0.0 copy-done.1
  142.7 4.3 %shard_map.115 = (f32[1152,128]{1,0:T(8,128)}, f32[384,128]{1,0:T(8,128)S(1)}, f32[384,128]{1,0:T(8,128)S(1)}) custom-call(f32[2304,128]{1,0:T(8,128)S(1)} %bitcast.20, f32[128,1152]{1,0:T(8,128)S(1)} %get-tuple-element.28.zhat, f32[1,1152]{1,0:T(1,128)S(1)} %get-tuple-element.34.zinv, f32[256,1152]{1,0:T(8,128)S(1)} %get-tuple-element.35.val, ...), custom_call_target="tpu_custom_call" | custom-call | tf_op jit(solution)/shard_map/pallas_call | solution.py:457
  147.0 0.0 copy-start.7
  147.0 1.5 collective-permute-start.2
  148.5 1.1 collective-permute-done.2
  149.6 11.5 %all_to_all.39 = f32[16,24,128]{2,1,0:T(8,128)S(1)} all-to-all(f32[16,24,128]{2,1,0:T(8,128)S(1)} %bitcast.30), channel_id=1, replica_groups={{0,8,16,24,32,40,48,56,64,72,80,88,96,104,112,120},{1,9,17,25,33,41,49,..., dimensions={0} | all-to-all | bytes 393216 | tf_op jit(solution)/shard_map/all_to_all | solution.py:343
  161.2 10.5 %all_to_all.40 = f32[8,24,128]{2,1,0:T(8,128)S(1)} all-to-all(f32[8,24,128]{2,1,0:T(8,128)S(1)} %broadcast_in_dim.4), channel_id=1, replica_groups={{0,128,2,130,4,132,6,134},{1,129,3,131,5,133,7,135},{8,136,10,138,12,14..., dimensions={0} | all-to-all | bytes 196608 | tf_op jit(solution)/shard_map/all_to_all | solution.py:343
  171.7 10.3 %all_to_all.41 = f32[16,24,128]{2,1,0:T(8,128)S(1)} all-to-all(f32[16,24,128]{2,1,0:T(8,128)S(1)} %broadcast_in_dim.5), channel_id=1, replica_groups={{0,8,16,24,32,40,48,56,64,72,80,88,96,104,112,120},{1,9,17,25,33,41,49,..., dimensions={0} | all-to-all | bytes 393216 | tf_op jit(solution)/shard_map/all_to_all | solution.py:343
  182.0 4.3 %collective-permute-start.3 = (f32[384,128]{1,0:T(8,128)S(1)}, f32[384,128]{1,0:T(8,128)S(1)}, u32[]{:S(2)}, u32[]{:S(2)}) collective-permute-start(f32[384,128]{1,0:T(8,128)S(1)} %bitcast.24), channel_id=1, source_target_pairs={{0,1},{1,0},{2,3},{3,2},{4,5},{5,4},{6,7},{7,6},{8,9},{9,8},{10,11... | collective-permute-start | bytes 589832 | tf_op jit(solution)/shard_map/ppermute | solution.py:347
  186.3 1.1 collective-permute-done.3.theirs
  187.4 0.0 copy-done.7
  187.4 1.0 shard_map.116
  (6 shorter events, 0.1 us)
Async XLA Ops:
  0.6 1.0 copy-start
  1.6 1.1 copy-start.3
  2.6 0.7 copy-start.6
  47.4 5.7 %copy-start.8 = (s32[1,192]{1,0:T(1,128)S(1)}, s32[1,192]{1,0:T(1,128)}, u32[]{:S(2)}) copy-start(s32[1,192]{1,0:T(1,128)} %mask.5) | copy-start | bytes 2308
  47.4 5.7 %collective-permute-start = (f32[1152,128]{1,0:T(8,128)S(1)}, f32[1152,128]{1,0:T(8,128)S(1)}, u32[]{:S(2)}, u32[]{:S(2)}) collective-permute-start(f32[1152,128]{1,0:T(8,128)S(1)} %slice_bitcast_fusion), channel_id=1, source_target_pairs={{0,1},{1,0},{2,3},{3,2},{4,5},{5,4},{6,7},{7,6},{8,9},{9,8},{10,11... | collective-permute-start | bytes 1769480 | tf_op jit(solution)/shard_map/ppermute | solution.py:347
  53.1 22.8 %copy-start.2 = (f32[1,6,192,128]{3,2,1,0:T(8,128)S(1)}, f32[1,6,192,128]{3,2,1,0:T(8,128)}, u32[]{:S(2)}) copy-start(f32[1,6,192,128]{3,2,1,0:T(8,128)} %param.8) | copy-start | bytes 1769476
  53.1 22.8 %copy-start.4 = (f32[128,128]{1,0:T(8,128)S(1)}, f32[128,128]{1,0:T(8,128)}, u32[]{:S(2)}) copy-start(f32[128,128]{1,0:T(8,128)} %w_gate.3) | copy-start | bytes 196612
  53.1 22.8 %copy-start.5 = (f32[128,128]{1,0:T(8,128)S(1)}, f32[128,128]{1,0:T(8,128)}, u32[]{:S(2)}) copy-start(f32[128,128]{1,0:T(8,128)} %w_out.3) | copy-start | bytes 196612
  104.8 2.4 %collective-permute-start.1 = (f32[1152,128]{1,0:T(8,128)S(1)}, f32[1152,128]{1,0:T(8,128)S(1)}, u32[]{:S(2)}, u32[]{:S(2)}) collective-permute-start(f32[1152,128]{1,0:T(8,128)S(1)} %get-tuple-element.33), channel_id=1, source_target_pairs={{0,1},{1,0},{2,3},{3,2},{4,5},{5,4},{6,7},{7,6},{8,9},{9,8},{10,11... | collective-permute-start | bytes 1769480 | tf_op jit(solution)/shard_map/ppermute | solution.py:347
  108.6 34.1 %copy-start.1 = (f32[128,512]{1,0:T(8,128)S(1)}, f32[128,512]{1,0:T(8,128)}, u32[]{:S(2)}) copy-start(f32[128,512]{1,0:T(8,128)} %w_in.5) | copy-start | bytes 786436
  147.0 40.4 %copy-start.7 = (f32[2,128]{1,0:T(2,128)S(1)}, f32[2,128]{1,0:T(2,128)}, u32[]{:S(2)}) copy-start(f32[2,128]{1,0:T(2,128)} %gains.7) | copy-start | bytes 3076
  147.0 2.6 %collective-permute-start.2 = (f32[384,128]{1,0:T(8,128)S(1)}, f32[384,128]{1,0:T(8,128)S(1)}, u32[]{:S(2)}, u32[]{:S(2)}) collective-permute-start(f32[384,128]{1,0:T(8,128)S(1)} %get-tuple-element.42), channel_id=1, source_target_pairs={{0,1},{1,0},{2,3},{3,2},{4,5},{5,4},{6,7},{7,6},{8,9},{9,8},{10,11... | collective-permute-start | bytes 589832 | tf_op jit(solution)/shard_map/ppermute | solution.py:347
  182.0 5.4 %collective-permute-start.3 = (f32[384,128]{1,0:T(8,128)S(1)}, f32[384,128]{1,0:T(8,128)S(1)}, u32[]{:S(2)}, u32[]{:S(2)}) collective-permute-start(f32[384,128]{1,0:T(8,128)S(1)} %bitcast.24), channel_id=1, source_target_pairs={{0,1},{1,0},{2,3},{3,2},{4,5},{5,4},{6,7},{7,6},{8,9},{9,8},{10,11... | collective-permute-start | bytes 589832 | tf_op jit(solution)/shard_map/ppermute | solution.py:347

commit v3 on v2

--- a/solution.py
+++ b/solution.py
@@ -124,7 +124,7 @@
     lax.fori_loop(0, pair.shape[0] // LANES, step, 0)
 
 
-def make_masks(mask, line, swap, n):
+def make_masks(mask, line, swap):
     res = mask.shape[1]
     line[...] = jnp.zeros_like(line)
     line[0:1, pl.ds(0, res)] = mask[...].astype(F32)
@@ -132,11 +132,11 @@
     both = across * across.T
     swap[0:256, :] = both[:, :128]
     swap[256:512, :] = both[:, 128:]
+
+
+def read_masks(swap, n, res):
     rows = res // n
     return [[swap[pl.ds(256 * half + il, n, stride=rows), :] for half in range(2)] for il in range(rows)]
-
-
-MASK_SCRATCH = [pltpu.VMEM((8, 256), F32), pltpu.VMEM((512, 128), F32)]
 
 
 def core_of():
@@ -148,11 +148,12 @@
     return jnp.where(first, mine, other), jnp.where(first, other, mine)
 
 
-def triangle_kernel(n, got, other, mask, send, a_out, b_out, line, swap):
+def triangle_kernel(n, got, other, mask, send, a_out, b_out, swap, line):
     per = got.shape[0] // (2 * 9 * n)
     res = mask.shape[1]
     rows = res // (2 * n)
-    pm = make_masks(mask, line, swap, n)
+    make_masks(mask, line, swap)
+    pm = read_masks(swap, n, res)
     for q in range(per):
         base = 512 * q
         for half in range(2):
@@ -184,14 +185,24 @@
                 send[tile_rows(n, per, 3 * p + t, q), :] = tile
 
 
-def output_kernel(n, res, got, up, zhat, w_gate, w_out, gains, send, dzn, mg, mo, wgt, wot):
-    hidden = w_out.shape[0]
-    per = hidden // n
+def gate_kernel(res, up, zhat, w_gate, w_out, gains, d_out, slope, grad, wgt):
     gain0, gain1 = column(gains[0:1, :]), column(gains[1:2, :])
     wgt[...] = w_gate[...].T
-    wot[...] = w_out[...].T
-    mg[...] = jnp.zeros_like(mg)
-    mo[...] = jnp.zeros_like(mo)
+
+    def step(c, _):
+        at = pl.ds(pl.multiple_of(c * LANES, LANES), LANES)
+        gate = jax.nn.sigmoid(dot3(parts(wgt[...]), parts(zhat[:, at] * gain0)))
+        passed = load_cells(up, c, res) * gate
+        d_out[:, at] = passed
+        slope[:, at] = passed * (1.0 - gate)
+        grad[:, at] = dot3(parts(w_out[...]), parts(passed)) * gain1
+        return 0
+
+    lax.fori_loop(0, up.shape[0] // LANES, step, 0)
+
+
+def norm_back_kernel(n, got, grad, send, xhat):
+    per = got.shape[0] // (9 * n)
 
     def step(c, _):
         at = pl.ds(pl.multiple_of(c * LANES, LANES), LANES)
@@ -202,25 +213,34 @@
             ],
             axis=1,
         )
-        xhat, inverse = hat(x)
-        z = zhat[:, at]
-        z_parts = parts(z)
-        upstream = load_cells(up, c, res)
-        gate = jax.nn.sigmoid(dot3(parts(wgt[...]), parts(z * gain0)))
-        out = dot3(parts(wot[...]), parts(xhat * gain1))
-        d_out = parts(upstream * gate)
-        d_logit = parts(upstream * out * gate * (1.0 - gate))
-        mo[...] += dot3(d_out, parts(xhat), NT)
-        mg[...] += dot3(d_logit, z_parts, NT)
-        dzn[:, at] = dot3(parts(w_gate[...]), d_logit)
-        g = dot3(parts(w_out[...]), d_out) * gain1
-        dx = hat_back(g, xhat, inverse)
+        normal, inverse = hat(x)
+        xhat[:, at] = normal
+        dx = hat_back(grad[:, at], normal, inverse)
         for q in range(per):
             for t in range(3):
                 send[tile_rows(n, per, 3 * c + t, q), :] = dx[q * n : (q + 1) * n, t * 128 : (t + 1) * 128]
         return 0
 
-    lax.fori_loop(0, up.shape[0] // LANES, step, 0)
+    lax.fori_loop(0, xhat.shape[1] // LANES, step, 0)
+
+
+def output_kernel(xhat, zhat, d_out, slope, w_gate, w_out, gains, dzn, mg, mo, wot):
+    gain1 = column(gains[1:2, :])
+    wot[...] = w_out[...].T
+    mg[...] = jnp.zeros_like(mg)
+    mo[...] = jnp.zeros_like(mo)
+
+    def step(c, _):
+        at = pl.ds(pl.multiple_of(c * LANES, LANES), LANES)
+        normal = xhat[:, at]
+        out = dot3(parts(wot[...]), parts(normal * gain1))
+        d_logit = parts(slope[:, at] * out)
+        mo[...] += dot3(parts(d_out[:, at]), parts(normal), NT)
+        mg[...] += dot3(d_logit, parts(zhat[:, at]), NT)
+        dzn[:, at] = dot3(parts(w_gate[...]), d_logit)
+        return 0
+
+    lax.fori_loop(0, xhat.shape[1] // LANES, step, 0)
 
 
 def gather_dx(n, got, q, dx_all):
@@ -233,11 +253,10 @@
     return parts(dx_all[...])
 
 
-def b_back_kernel(n, got, mask, a_in, keep, give, line, swap, dx_all, db_all):
+def b_back_kernel(n, res, got, swap, a_in, keep, give, dx_all, db_all):
     per = got.shape[0] // (9 * n)
-    res = mask.shape[1]
     rows = res // (2 * n)
-    pm = make_masks(mask, line, swap, n)
+    pm = read_masks(swap, n, res)
     for q in range(per):
         db = dot3(gather_dx(n, got, q, dx_all), parts(a_in[q]), TN)
         db_all[0:256, :] = db[:, :128]
@@ -256,11 +275,10 @@
                 keep[at, :], give[at, :] = by_core(tiles[0][t], tiles[1][t])
 
 
-def a_back_kernel(n, got, mask, b_in, keep, taken, send, line, swap, dx_all):
+def a_back_kernel(n, res, got, swap, b_in, send, dx_all):
     per = got.shape[0] // (9 * n)
-    res = mask.shape[1]
     rows = res // (2 * n)
-    pm = make_masks(mask, line, swap, n)
+    pm = read_masks(swap, n, res)
     for q in range(per):
         base = 512 * q
         b_whole = jnp.concatenate([b_in[pl.ds(base, 256), :], b_in[pl.ds(base + 256, 256), :]], axis=1)
@@ -271,51 +289,68 @@
                 own = [by_core(pm[il][half], pm[rows + il][half])[0] for half in range(2)]
                 two.append([da[il * n : (il + 1) * n, 128 * half : 128 * half + 128] * own[half] for half in range(2)])
             for t, tile in enumerate(to_tiles(*two)):
-                at = tile_rows(n, per, 3 * p + t, q)
                 send[tile_rows(n, 2 * per, 3 * p + t, q), :] = tile
-                send[tile_rows(n, 2 * per, 3 * p + t, per + q), :] = keep[at, :] + taken[at, :]
-
-
-def input_kernel(n, res, got, zhat, zinv, val, sig, dzn, w_in, gains, mg, mo, d_pair, keep, give, mi, w_hi, w_lo):
-    hidden = w_in.shape[1] // 4
+
+
+def add_kernel(half_sent, keep, taken, send):
+    per = keep.shape[1]
+    send[:, :per, :] = half_sent[:, :per, :]
+    send[:, per:, :] = keep[...] + taken[...]
+
+
+def read_grads(n, got, val, sig, c, which):
+    hidden = val.shape[0] // 2
     per = hidden // n
-    wh, wl = parts(w_in[...])
-    w_hi[...], w_lo[...] = wh, wl
-    gain0 = column(gains[0:1, :])
+    at = pl.ds(pl.multiple_of(c * LANES, LANES), LANES)
+    d = jnp.concatenate(
+        [
+            jnp.concatenate([got[tile_rows(n, 2 * per, 3 * c + t, which * per + q), :] for q in range(per)], axis=0)
+            for t in range(3)
+        ],
+        axis=1,
+    )
+    rows = pl.ds(which * hidden, hidden)
+    gate = sig[rows, at]
+    d_val = d * gate
+    return d_val, d_val * val[rows, at] * (1.0 - gate)
+
+
+def weight_kernel(n, got, zhat, val, sig, mg, mo, keep, give, mi):
+    hidden = val.shape[0] // 2
     mi[...] = jnp.zeros_like(mi)
 
     def step(c, _):
         at = pl.ds(pl.multiple_of(c * LANES, LANES), LANES)
-        z = zhat[:, at]
-        z_parts = parts(z)
-        total = dzn[:, at]
+        z = parts(zhat[:, at])
         for which in range(2):
-            d = jnp.concatenate(
-                [
-                    jnp.concatenate(
-                        [got[tile_rows(n, 2 * per, 3 * c + t, which * per + q), :] for q in range(per)], axis=0
-                    )
-                    for t in range(3)
-                ],
-                axis=1,
-            )
-            rows = pl.ds(which * hidden, hidden)
-            gate = sig[rows, at]
-            d_val = d * gate
-            d_gate = d_val * val[rows, at] * (1.0 - gate)
-            for k, grad in ((2 * which, d_val), (2 * which + 1, d_gate)):
-                cols = pl.ds(k * hidden, hidden)
-                grad = parts(grad)
-                total += dot3((w_hi[:, cols], w_lo[:, cols]), grad)
-                mi[cols, :] += dot3(grad, z_parts, NT)
-        store_cells(d_pair, c, res, hat_back(total * gain0, z, zinv[:, at]))
+            for k, grad in enumerate(read_grads(n, got, val, sig, c, which)):
+                mi[pl.ds((2 * which + k) * hidden, hidden), :] += dot3(parts(grad), z, NT)
         return 0
 
-    lax.fori_loop(0, d_pair.shape[0] // LANES, step, 0)
+    lax.fori_loop(0, zhat.shape[1] // LANES, step, 0)
     half = keep.shape[0]
     low = mi[pl.ds(0, half), :]
     high = jnp.concatenate([mi[pl.ds(half, mi.shape[0] - half), :], mg[...], mo[...]], axis=0)
     keep[...], give[...] = by_core(low, high)
+
+
+def input_kernel(n, res, got, zhat, zinv, val, sig, dzn, w_in, gains, d_pair, w_hi, w_lo):
+    hidden = val.shape[0] // 2
+    wh, wl = parts(w_in[...])
+    w_hi[...], w_lo[...] = wh, wl
+    gain0 = column(gains[0:1, :])
+
+    def step(c, _):
+        at = pl.ds(pl.multiple_of(c * LANES, LANES), LANES)
+        total = dzn[:, at]
+        for which in range(2):
+            for k, grad in enumerate(read_grads(n, got, val, sig, c, which)):
+                cols = pl.ds((2 * which + k) * hidden, hidden)
+                total += dot3((w_hi[:, cols], w_lo[:, cols]), parts(grad))
+        store_cells(d_pair, c, res, hat_back(total * gain0, zhat[:, at], zinv[:, at]))
+        return 0
+
+    lax.fori_loop(0, d_pair.shape[0] // LANES, step, 0)
 
 
 def finish_kernel(mine, theirs, w_in, w_gate, w_out, gains, d_w_in, d_w_gate, d_w_out, d_gains, m):
@@ -386,8 +421,7 @@
     in_plane, in_line = len(planes[0]), len(lines[0])
     mine = summed(keep + swap_cores(give, n), planes, in_plane)
     mine = summed(spread(mine, in_line), lines, in_line)
-    mine = exchange(spread(mine, in_plane), BOTH, planes).reshape(count, width)
-    return mine, swap_cores(mine, n)
+    return exchange(spread(mine, in_plane), BOTH, planes).reshape(count, width)
 
 
 def shards(devices, n_dp, pair, upstream, residue_mask, w_in, w_gate, w_out, gains):
@@ -407,59 +441,78 @@
     def narrow(x):
         return exchange(x.reshape(n, 9 * per, 128), "dap", same_core).reshape(tiles, 128)
 
+    flat = (width, cells)
+    product = 6 * width * hidden * cells
+
     send, zhat, zinv, val, sig = call(
         functools.partial(project_kernel, n, res),
-        [
-            ((2 * tiles, 128), F32),
-            ((width, cells), F32),
-            ((1, cells), F32),
-            ((2 * hidden, cells), F32),
-            ((2 * hidden, cells), F32),
-        ],
+        [((2 * tiles, 128), F32), (flat, F32), ((1, cells), F32), ((2 * hidden, cells), F32), ((2 * hidden, cells), F32)],
         [pltpu.VMEM((4 * hidden, width), BF16)] * 2,
     )(pair2, w_in, gains)
     got = wide(send)
 
     other = swap_cores(got.reshape(n * 9, 2, per, 128)[:, 1].reshape(tiles, 128), n)
-    send, a_all, b_all = call(
+    up2, _ = lax.optimization_barrier((up2, got))
+    d_out, slope, grad = call(
+        functools.partial(gate_kernel, res),
+        [(flat, F32)] * 3,
+        [pltpu.VMEM((width, width), F32)],
+        flops=2 * product,
+        moved=4 * cells * width * 5,
+    )(up2, zhat, w_gate, w_out, gains)
+    send, a_all, b_all, pm = call(
         functools.partial(triangle_kernel, n),
-        [((tiles, 128), F32), ((per, res // 2, 256), F32), ((per * 512, 128), F32)],
-        MASK_SCRATCH,
+        [((tiles, 128), F32), ((per, res // 2, 256), F32), ((per * 512, 128), F32), ((512, 128), F32)],
+        [pltpu.VMEM((8, 256), F32)],
     )(got, other, residue_mask)
     got = narrow(send)
 
-    send, dzn, mg, mo = call(
-        functools.partial(output_kernel, n, res),
-        [
-            ((tiles, 128), F32),
-            ((width, cells), F32),
-            ((width, width), F32),
-            ((width, hidden), F32),
-        ],
-        [pltpu.VMEM((width, width), F32), pltpu.VMEM((width, hidden), F32)],
-    )(got, up2, zhat, w_gate, w_out, gains)
+    send, xhat = call(functools.partial(norm_back_kernel, n), [((tiles, 128), F32), (flat, F32)])(got, grad)
     got = narrow(send)
 
     keep, give = call(
-        functools.partial(b_back_kernel, n),
+        functools.partial(b_back_kernel, n, res),
         [((tiles, 128), F32)] * 2,
-        MASK_SCRATCH + [pltpu.VMEM((res // 2, 256), F32), pltpu.VMEM((512, 128), F32)],
-    )(got, residue_mask, a_all)
+        [pltpu.VMEM((res // 2, 256), F32), pltpu.VMEM((512, 128), F32)],
+    )(got, pm, a_all)
+    give, got, xhat = lax.optimization_barrier((give, got, xhat))
     taken = swap_cores(give, n)
     (send,) = call(
-        functools.partial(a_back_kernel, n),
+        functools.partial(a_back_kernel, n, res),
         [((2 * tiles, 128), F32)],
-        MASK_SCRATCH + [pltpu.VMEM((res // 2, 256), F32)],
-    )(got, residue_mask, b_all, keep, taken)
+        [pltpu.VMEM((res // 2, 256), F32)],
+        flops=product,
+        moved=4 * cells * width * 4,
+    )(got, pm, b_all)
+    dzn, mg, mo = call(
+        output_kernel,
+        [(flat, F32), ((width, width), F32), ((width, hidden), F32)],
+        [pltpu.VMEM((width, hidden), F32)],
+        flops=4 * product,
+        moved=4 * cells * width * 5,
+    )(xhat, zhat, d_out, slope, w_gate, w_out, gains)
+    group = (n * 9, per, 128)
+    (send,) = call(add_kernel, [((n * 9, 2 * per, 128), F32)])(
+        send.reshape(n * 9, 2 * per, 128), keep.reshape(group), taken.reshape(group)
+    )
     got = wide(send)
 
     half = (4 * hidden + 2 * width) // 2
-    d_pair, keep, give = call(
+    keep, give = call(
+        functools.partial(weight_kernel, n),
+        [((half, width), F32), ((half, width), F32)],
+        [pltpu.VMEM((4 * hidden, width), F32)],
+    )(got, zhat, val, sig, mg, mo)
+    mine = reduce_all(keep, give, n, n_dp)
+    mine, got = lax.optimization_barrier((mine, got))
+    theirs = swap_cores(mine, n)
+    (d_pair,) = call(
         functools.partial(input_kernel, n, res),
-        [((cells, width), F32), ((half, width), F32), ((half, width), F32)],
-        [pltpu.VMEM((4 * hidden, width), F32)] + [pltpu.VMEM((width, 4 * hidden), BF16)] * 2,
-    )(got, zhat, zinv, val, sig, dzn, w_in, gains, mg, mo)
-    mine, theirs = reduce_all(keep, give, n, n_dp)
+        [((cells, width), F32)],
+        [pltpu.VMEM((width, 4 * hidden), BF16)] * 2,
+        flops=4 * product,
+        moved=4 * cells * width * 7,
+    )(got, zhat, zinv, val, sig, dzn, w_in, gains)
 
     d_w_in, d_w_gate, d_w_out, d_gains = call(
         finish_kernel,

time: 189 us -> 197 us (1.042)
  blocking collectives: 154 us -> 97.3 us
  waiting for transfers between devices: 5.4 us -> 42.4 us
  local copies, waits for them, and re-layouts: 2.77 us -> 16.9 us
  starting transfers between devices: 10.6 us -> 18.7 us
  Pallas kernels: 15.1 us -> 19.3 us
    all_to_all x7 -> x5, blocking collectives: 154 us -> 97.3 us  [exchange(): return lax.all_to_all(x, axis, 0, 0, tiled=True, axis_index_groups=groups)]
    all_to_all x0 -> x2, waiting for transfers between devices: none -> 39.2 us  [exchange(): return lax.all_to_all(x, axis, 0, 0, tiled=True, axis_index_groups=groups)]
    unnamed x18 -> x48, local copies, waits for them, and re-layouts: 2.71 us -> 16.1 us
    all_to_all x0 -> x2, starting transfers between devices: none -> 7.28 us  [exchange(): return lax.all_to_all(x, axis, 0, 0, tiled=True, axis_index_groups=groups)]
    pallas_call x4 -> x8, Pallas kernels: 10 us -> 13.4 us  [the longest x1 3.12 us: shards(): call(functools.partial(input_kernel, n, res), [((cells, width), F32)], [p...]
    ppermute x4, waiting for transfers between devices: 5.4 us -> 3.26 us  [swap_cores(): return lax.ppermute(x, 'dap', [(i, i ^ 1) for i in range(2 * n)])]
  transfers between devices with their start and end apart: 4 -> 6, of which waited for: 4 -> 5; matrix products, arithmetic and copies ran while one was open for 0% -> 0% of each run, Pallas kernels for 0% -> 4%
where the time goes in v3:
time: 197 us; the launch traced here: 196 us
  blocking collectives  97.3 us (49%)
  waiting for transfers between devices  42.4 us (22%)
  Pallas kernels  19.3 us (10%)
  starting transfers between devices  18.7 us (9%)
  local copies, waits for them, and re-layouts  16.9 us (9%)
    all_to_all x5, blocking collectives, exchange(): return lax.all_to_all(x, axis, 0, 0, tiled=True, axis_index_groups=groups)  97.3 us
    all_to_all x2, waiting for transfers between devices, exchange(): return lax.all_to_all(x, axis, 0, 0, tiled=True, axis_index_groups=groups)  39.2 us
    unnamed x48, local copies, waits for them, and re-layouts  16.1 us
    ppermute x4, starting transfers between devices, swap_cores(): return lax.ppermute(x, 'dap', [(i, i ^ 1) for i in range(2 * n)])  11.4 us
    all_to_all x2, starting transfers between devices, exchange(): return lax.all_to_all(x, axis, 0, 0, tiled=True, axis_index_groups=groups)  7.28 us
  transfers between devices with their start and end apart: 6, of which 5 were waited for; matrix products, arithmetic and copies ran while one was open for 0% of the time, Pallas kernels for 4%

profile of v3, /device:TPU:1, one launch (start us, length us, event | category | flops | bytes accessed | tf_op | source)
XLA Modules:
  0.0 196.0 jit_solution(7065668247185604533)
XLA Ops:
  0.6 0.0 copy-start.3
  0.6 0.9 copy-done.3
  1.6 0.0 copy-start.11
  1.6 1.1 copy-done.11
  2.6 0.0 copy-start.21
  2.7 0.7 copy-done.21
  3.3 2.3 %shard_map.110 = (f32[2304,128]{1,0:T(8,128)S(1)}, f32[128,1152]{1,0:T(8,128)S(1)}, f32[1,1152]{1,0:T(1,128)S(1)}, f32[256,1152]{1,0:T(8,128)S(1)}, f32[256,1152]{1,0:T(8,128)S(1)}) custom-call(f32[1152,128]{1,0:T(8,128)S(1)} %bitcast.32, f32[128,512]{1,0:T(8,128)S(1)} %copy-done.3, f32[2,128]{1,0:T(2,128)S(1)} %copy-done.21), custom_call_target="tpu_custom_call" | custom-call | tf_op jit(solution)/shard_map/pallas_call | solution.py:447
  5.7 0.0 copy-start
  5.7 41.6 %all_to_all.35 = f32[16,144,128]{2,1,0:T(8,128)S(1)} all-to-all(f32[16,144,128]{2,1,0:T(8,128)S(1)} %bitcast.27), channel_id=1, replica_groups={{0,2,4,6,8,10,12,14,16,18,20,22,24,26,28,30},{1,3,5,7,9,11,13,15,17,19,..., dimensions={0} | all-to-all | bytes 2359296 | tf_op jit(solution)/shard_map/all_to_all | solution.py:378
  47.3 0.0 copy-done
  47.3 4.2 %collective-permute-start = (f32[1152,128]{1,0:T(8,128)S(1)}, f32[1152,128]{1,0:T(8,128)S(1)}, u32[]{:S(2)}, u32[]{:S(2)}) collective-permute-start(f32[1152,128]{1,0:T(8,128)S(1)} %slice_bitcast_fusion), channel_id=1, source_target_pairs={{0,1},{1,0},{2,3},{3,2},{4,5},{5,4},{6,7},{7,6},{8,9},{9,8},{10,11... | collective-permute-start | bytes 1769480 | tf_op jit(solution)/shard_map/ppermute | solution.py:382
  51.5 1.6 collective-permute-done.other
  53.1 0.0 copy-done.23
  53.2 2.5 %shard_map.111 = (f32[1152,128]{1,0:T(8,128)}, f32[8,96,256]{2,1,0:T(8,128)S(1)}, f32[4096,128]{1,0:T(8,128)S(1)}, f32[512,128]{1,0:T(8,128)S(1)}) custom-call(f32[2304,128]{1,0:T(8,128)S(1)} %bitcast.22, f32[1152,128]{1,0:T(8,128)S(1)} %collective-permute-done.other, s32[1,192]{1,0:T(1,128)S(1)} %copy-done.23), custom_call_target="tpu_custom_call" | custom-call | tf_op jit(solution)/shard_map/pallas_call | solution.py:463
  55.7 1.3 copy-done.5
  57.1 0.9 copy-done.7
  57.9 3.6 %all-to-all-start.1 = ((f32[16,72,128]{2,1,0:T(8,128)}), f32[16,72,128]{2,1,0:T(8,128)S(1)}, u32[]{:S(2)}, u32[]{:S(2)}) async-start(f32[16,72,128]{2,1,0:T(8,128)} %bitcast.5), calls=%async_computation.1 | async-start | bytes 1179648 | tf_op jit(solution)/shard_map/all_to_all | solution.py:378
  61.5 0.0 copy-done.9
  61.5 0.0 copy-done.10
  61.5 0.0 copy-done.22
  61.6 0.0 copy-start.12
  61.6 1.1 copy-done.12
  62.6 1.9 shard_map.112
  64.5 0.0 copy-start.15
  64.5 0.8 copy-done.15
  65.4 0.8 copy-done.17
  66.2 14.1 %all-to-all-done.1 = f32[16,72,128]{2,1,0:T(8,128)S(1)} async-done(((f32[16,72,128]{2,1,0:T(8,128)}), f32[16,72,128]{2,1,0:T(8,128)S(1)}, u32[]{:S(2)}, u32[]{:S(2)}) %all-to-all-start.1) | async-done | bytes 589856 | tf_op jit(solution)/shard_map/all_to_all | solution.py:378
  80.3 0.4 shard_map.113
  80.7 0.0 copy-start.19
  80.8 0.8 copy-done.19
  81.6 22.6 %all_to_all.36 = f32[16,72,128]{2,1,0:T(8,128)S(1)} all-to-all(f32[16,72,128]{2,1,0:T(8,128)S(1)} %bitcast.34), channel_id=1, replica_groups={{0,2,4,6,8,10,12,14,16,18,20,22,24,26,28,30},{1,3,5,7,9,11,13,15,17,19,..., dimensions={0} | all-to-all | bytes 1179648 | tf_op jit(solution)/shard_map/all_to_all | solution.py:378
  104.2 0.0 copy-done.8
  104.2 1.4 shard_map.114
  105.6 0.7 collective-permute-start.1
  106.3 0.0 copy-done.6
  106.3 1.1 shard_map.115
  107.4 0.6 collective-permute-done.1
  108.0 1.1 shard_map.116
  109.1 3.7 %all-to-all-start.3 = ((f32[16,144,128]{2,1,0:T(8,128)}), f32[16,144,128]{2,1,0:T(8,128)S(1)}, u32[]{:S(2)}, u32[]{:S(2)}) async-start(f32[16,144,128]{2,1,0:T(8,128)} %bitcast.13), calls=%async_computation.3 | async-start | bytes 2359296 | tf_op jit(solution)/shard_map/all_to_all | solution.py:378
  112.8 0.0 copy-start.16
  112.8 1.1 copy-done.16
  113.9 1.1 copy-done.18
  114.9 1.1 copy-done.20
  116.0 2.1 %shard_map.117 = (f32[128,1152]{1,0:T(8,128)S(1)}, f32[128,128]{1,0:T(8,128)S(1)}, f32[128,128]{1,0:T(8,128)S(1)}) custom-call(f32[128,1152]{1,0:T(8,128)S(1)} %copy-done.20, f32[128,1152]{1,0:T(8,128)S(1)} %get-tuple-element.39.zhat, f32[128,1152]{1,0:T(8,128)S(1)} %copy-done.16, f32[128,1152]{1,0:T(8,128)S(1)} %copy-done.18, f32[128,128]{1,0:T(8,128)S(1)} %copy-done.9, ...), custom_call_target="tpu_custom_call" | custom-call | flops 452984832 | bytes 2949120 | tf_op jit(solution)/shard_map/pallas_call | solution.py:487
  118.1 0.0 copy-start.13
  118.1 0.8 copy-done.13
  118.9 25.1 %all-to-all-done.3 = f32[16,144,128]{2,1,0:T(8,128)S(1)} async-done(((f32[16,144,128]{2,1,0:T(8,128)}), f32[16,144,128]{2,1,0:T(8,128)S(1)}, u32[]{:S(2)}, u32[]{:S(2)}) %all-to-all-start.3) | async-done | bytes 1179680 | tf_op jit(solution)/shard_map/all_to_all | solution.py:378
  144.0 1.3 copy-done.1
  145.3 2.2 %shard_map.118 = (f32[384,128]{1,0:T(8,128)S(1)}, f32[384,128]{1,0:T(8,128)S(1)}) custom-call(f32[2304,128]{1,0:T(8,128)S(1)} %bitcast.19, f32[128,1152]{1,0:T(8,128)S(1)} %get-tuple-element.39.zhat, f32[256,1152]{1,0:T(8,128)S(1)} %get-tuple-element.50.val, f32[256,1152]{1,0:T(8,128)S(1)} %copy-done.1, f32[128,128]{1,0:T(8,128)S(1)} %get-tuple-element.55.mg, ...), custom_call_target="tpu_custom_call" | custom-call | tf_op jit(solution)/shard_map/pallas_call | solution.py:501
  147.5 0.0 copy-start.4
  147.5 2.2 %collective-permute-start.2 = (f32[384,128]{1,0:T(8,128)S(1)}, f32[384,128]{1,0:T(8,128)S(1)}, u32[]{:S(2)}, u32[]{:S(2)}) collective-permute-start(f32[384,128]{1,0:T(8,128)S(1)} %get-tuple-element.58), channel_id=1, source_target_pairs={{0,1},{1,0},{2,3},{3,2},{4,5},{5,4},{6,7},{7,6},{8,9},{9,8},{10,11... | collective-permute-start | bytes 589832 | tf_op jit(solution)/shard_map/ppermute | solution.py:382
  149.7 1.1 collective-permute-done.2
  150.8 11.3 %all_to_all.37 = f32[16,24,128]{2,1,0:T(8,128)S(1)} all-to-all(f32[16,24,128]{2,1,0:T(8,128)S(1)} %bitcast.35), channel_id=1, replica_groups={{0,8,16,24,32,40,48,56,64,72,80,88,96,104,112,120},{1,9,17,25,33,41,49,..., dimensions={0} | all-to-all | bytes 393216 | tf_op jit(solution)/shard_map/all_to_all | solution.py:378
  162.1 0.6 reduce_sum.18
  162.7 0.7 broadcast_in_dim.4
  163.4 11.6 %all_to_all.38 = f32[8,24,128]{2,1,0:T(8,128)S(1)} all-to-all(f32[8,24,128]{2,1,0:T(8,128)S(1)} %broadcast_in_dim.4), channel_id=1, replica_groups={{0,128,2,130,4,132,6,134},{1,129,3,131,5,133,7,135},{8,136,10,138,12,14..., dimensions={0} | all-to-all | bytes 196608 | tf_op jit(solution)/shard_map/all_to_all | solution.py:378
  175.0 10.3 %all_to_all.39 = f32[16,24,128]{2,1,0:T(8,128)S(1)} all-to-all(f32[16,24,128]{2,1,0:T(8,128)S(1)} %broadcast_in_dim.5), channel_id=1, replica_groups={{0,8,16,24,32,40,48,56,64,72,80,88,96,104,112,120},{1,9,17,25,33,41,49,..., dimensions={0} | all-to-all | bytes 393216 | tf_op jit(solution)/shard_map/all_to_all | solution.py:378
  185.3 4.3 %collective-permute-start.3 = (f32[384,128]{1,0:T(8,128)S(1)}, f32[384,128]{1,0:T(8,128)S(1)}, u32[]{:S(2)}, u32[]{:S(2)}) collective-permute-start(f32[384,128]{1,0:T(8,128)S(1)} %bitcast.28), channel_id=1, source_target_pairs={{0,1},{1,0},{2,3},{3,2},{4,5},{5,4},{6,7},{7,6},{8,9},{9,8},{10,11... | collective-permute-start | bytes 589832 | tf_op jit(solution)/shard_map/ppermute | solution.py:382
  189.6 0.0 copy-done.4
  189.6 1.3 copy-done.2
  190.9 1.1 copy-done.14
  191.9 3.1 %shard_map.119 = f32[1152,128]{1,0:T(8,128)} custom-call(f32[2304,128]{1,0:T(8,128)S(1)} %bitcast.20, f32[128,1152]{1,0:T(8,128)S(1)} %get-tuple-element.39.zhat, f32[1,1152]{1,0:T(1,128)S(1)} %get-tuple-element.60.zinv, f32[256,1152]{1,0:T(8,128)S(1)} %get-tuple-element.50.val, f32[256,1152]{1,0:T(8,128)S(1)} %copy-done.2, f32[128,1152]{1,0:T(8,128)S(1)} %copy-done.14, ...), custom_call_target="tpu_custom_call" | custom-call | flops 452984832 | bytes 4128768 | tf_op jit(solution)/shard_map/pallas_call | solution.py:509
  195.0 0.0 collective-permute-done.3.theirs
  195.0 1.0 shard_map.120
  (18 shorter events, 0.1 us)
Async XLA Ops:
  0.6 1.0 copy-start.3
  1.6 1.1 copy-start.11
  2.6 0.7 copy-start.21
  5.7 41.6 %copy-start = (f32[256,1152]{1,0:T(8,128)}, f32[256,1152]{1,0:T(8,128)S(1)}, u32[]{:S(2)}) copy-start(f32[256,1152]{1,0:T(8,128)S(1)} %get-tuple-element.51.sig) | copy-start | bytes 3538948
  47.3 5.9 %copy-start.23 = (s32[1,192]{1,0:T(1,128)S(1)}, s32[1,192]{1,0:T(1,128)}, u32[]{:S(2)}) copy-start(s32[1,192]{1,0:T(1,128)} %mask.1) | copy-start | bytes 2308
  47.3 5.8 %collective-permute-start = (f32[1152,128]{1,0:T(8,128)S(1)}, f32[1152,128]{1,0:T(8,128)S(1)}, u32[]{:S(2)}, u32[]{:S(2)}) collective-permute-start(f32[1152,128]{1,0:T(8,128)S(1)} %slice_bitcast_fusion), channel_id=1, source_target_pairs={{0,1},{1,0},{2,3},{3,2},{4,5},{5,4},{6,7},{7,6},{8,9},{9,8},{10,11... | collective-permute-start | bytes 1769480 | tf_op jit(solution)/shard_map/ppermute | solution.py:382
  53.2 8.4 %copy-start.9 = (f32[128,128]{1,0:T(8,128)S(1)}, f32[128,128]{1,0:T(8,128)}, u32[]{:S(2)}) copy-start(f32[128,128]{1,0:T(8,128)} %w_gate.5) | copy-start | bytes 196612
  53.2 8.4 %copy-start.10 = (f32[128,128]{1,0:T(8,128)S(1)}, f32[128,128]{1,0:T(8,128)}, u32[]{:S(2)}) copy-start(f32[128,128]{1,0:T(8,128)} %w_out.5) | copy-start | bytes 196612
  53.2 8.4 %copy-start.22 = (f32[2,128]{1,0:T(2,128)S(1)}, f32[2,128]{1,0:T(2,128)}, u32[]{:S(2)}) copy-start(f32[2,128]{1,0:T(2,128)} %gains.9) | copy-start | bytes 3076
  55.7 1.4 copy-start.5
  57.1 0.9 copy-start.7
  57.9 22.4 %all-to-all-start.1 = ((f32[16,72,128]{2,1,0:T(8,128)}), f32[16,72,128]{2,1,0:T(8,128)S(1)}, u32[]{:S(2)}, u32[]{:S(2)}) async-start(f32[16,72,128]{2,1,0:T(8,128)} %bitcast.5), calls=%async_computation.1 | async-start | bytes 1179648 | tf_op jit(solution)/shard_map/all_to_all | solution.py:378
  61.6 1.1 copy-start.12
  64.5 0.8 copy-start.15
  65.4 0.8 copy-start.17
  80.3 23.9 %copy-start.8 = (f32[8,96,256]{2,1,0:T(8,128)S(1)}, f32[8,96,256]{2,1,0:T(8,128)}, u32[]{:S(2)}) copy-start(f32[8,96,256]{2,1,0:T(8,128)} %copy-done.7) | copy-start | bytes 2359300
  80.7 0.8 copy-start.19
  81.6 24.8 %copy-start.6 = (f32[4096,128]{1,0:T(8,128)S(1)}, f32[4096,128]{1,0:T(8,128)}, u32[]{:S(2)}) copy-start(f32[4096,128]{1,0:T(8,128)} %copy-done.5) | copy-start | bytes 6291460
  105.6 2.3 %collective-permute-start.1 = (f32[1152,128]{1,0:T(8,128)S(1)}, f32[1152,128]{1,0:T(8,128)S(1)}, u32[]{:S(2)}, u32[]{:S(2)}) collective-permute-start(f32[1152,128]{1,0:T(8,128)S(1)} %get-tuple-element.49), channel_id=1, source_target_pairs={{0,1},{1,0},{2,3},{3,2},{4,5},{5,4},{6,7},{7,6},{8,9},{9,8},{10,11... | collective-permute-start | bytes 1769480 | tf_op jit(solution)/shard_map/ppermute | solution.py:382
  109.1 34.9 %all-to-all-start.3 = ((f32[16,144,128]{2,1,0:T(8,128)}), f32[16,144,128]{2,1,0:T(8,128)S(1)}, u32[]{:S(2)}, u32[]{:S(2)}) async-start(f32[16,144,128]{2,1,0:T(8,128)} %bitcast.13), calls=%async_computation.3 | async-start | bytes 2359296 | tf_op jit(solution)/shard_map/all_to_all | solution.py:378
  112.8 1.1 copy-start.16
  113.9 1.1 copy-start.18
  114.9 1.1 copy-start.20
  118.1 0.8 copy-start.13
  144.0 1.3 copy-start.1
  147.5 42.1 %copy-start.4 = (f32[128,512]{1,0:T(8,128)S(1)}, f32[128,512]{1,0:T(8,128)}, u32[]{:S(2)}) copy-start(f32[128,512]{1,0:T(8,128)} %w_in.5) | copy-start | bytes 786436
  147.5 3.2 %collective-permute-start.2 = (f32[384,128]{1,0:T(8,128)S(1)}, f32[384,128]{1,0:T(8,128)S(1)}, u32[]{:S(2)}, u32[]{:S(2)}) collective-permute-start(f32[384,128]{1,0:T(8,128)S(1)} %get-tuple-element.58), channel_id=1, source_target_pairs={{0,1},{1,0},{2,3},{3,2},{4,5},{5,4},{6,7},{7,6},{8,9},{9,8},{10,11... | collective-permute-start | bytes 589832 | tf_op jit(solution)/shard_map/ppermute | solution.py:382
  185.3 9.8 %collective-permute-start.3 = (f32[384,128]{1,0:T(8,128)S(1)}, f32[384,128]{1,0:T(8,128)S(1)}, u32[]{:S(2)}, u32[]{:S(2)}) collective-permute-start(f32[384,128]{1,0:T(8,128)S(1)} %bitcast.28), channel_id=1, source_target_pairs={{0,1},{1,0},{2,3},{3,2},{4,5},{5,4},{6,7},{7,6},{8,9},{9,8},{10,11... | collective-permute-start | bytes 589832 | tf_op jit(solution)/shard_map/ppermute | solution.py:382
  189.6 1.3 copy-start.2
  190.8 1.1 copy-start.14

commit v4 on v3

--- a/solution.py
+++ b/solution.py
@@ -31,6 +31,29 @@
 TN = ((0,), (0,))
 
 
+def stack_left(x):
+    hi, lo = parts(x)
+    return jnp.concatenate(
+        [jnp.concatenate([hi, hi], axis=1), jnp.concatenate([lo, jnp.zeros_like(lo)], axis=1)], axis=0
+    )
+
+
+def stack_rows(x):
+    return jnp.concatenate(parts(x), axis=0)
+
+
+def dot_stacked(left, right):
+    both = jnp.dot(left, right, preferred_element_type=F32)
+    m = left.shape[0] // 2
+    return both[:m] + both[m:]
+
+
+def dot_cells(left, right):
+    both = lax.dot_general(left, right, (NT, ((), ())), preferred_element_type=F32)
+    m, n = left.shape[0] // 2, right.shape[0] // 2
+    return both[:m, :n] + both[:m, n:] + both[m:, :n]
+
+
 def column(row):
     n = row.shape[1]
     return jnp.broadcast_to(row, (n, n)).T[:, :1]
@@ -53,7 +76,7 @@
         body,
         out_shape=[jax.ShapeDtypeStruct(s, d) for s, d in outs],
         scratch_shapes=list(scratch),
-        compiler_params=pltpu.CompilerParams(vmem_limit_bytes=40 * 2**20),
+        compiler_params=pltpu.CompilerParams(vmem_limit_bytes=16 * 2**20),
         cost_estimate=pl.CostEstimate(flops=flops, bytes_accessed=moved, transcendentals=0),
     )
 
@@ -93,11 +116,11 @@
     return even[0], jnp.where(low, even[1], pltpu.roll(odd[1], 64, 1)), odd[0]
 
 
-def project_kernel(n, res, pair, w_in, gains, send, zhat, zinv, val, sig, wt_hi, wt_lo):
+def project_kernel(n, res, pair, w_in, gains, send, zhat, zinv, val, sig, wt):
     hidden = w_in.shape[1] // 4
     per = hidden // n
     wh, wl = parts(w_in[...].T)
-    wt_hi[...], wt_lo[...] = wh, wl
+    wt[...] = jnp.concatenate([wh, wl, wh], axis=1)
     gain = column(gains[0:1, :])
 
     def step(c, _):
@@ -105,12 +128,12 @@
         z, inverse = hat(load_cells(pair, c, res))
         zhat[:, at] = z
         zinv[:, at] = inverse
-        zn = parts(z * gain)
+        zh, zl = parts(z * gain)
+        zn = jnp.concatenate([zh, zh, zl], axis=0)
         for which in range(2):
-            rows = pl.ds(2 * which * hidden, hidden)
-            gate_rows = pl.ds((2 * which + 1) * hidden, hidden)
-            value = dot3((wt_hi[rows, :], wt_lo[rows, :]), zn)
-            gate = jax.nn.sigmoid(dot3((wt_hi[gate_rows, :], wt_lo[gate_rows, :]), zn))
+            rows = pl.ds(2 * which * hidden, 2 * hidden)
+            proj = jnp.dot(wt[rows, :], zn, preferred_element_type=F32)
+            value, gate = proj[:hidden], jax.nn.sigmoid(proj[hidden:])
             val[pl.ds(which * hidden, hidden), at] = value
             sig[pl.ds(which * hidden, hidden), at] = gate
             both = value * gate
@@ -185,17 +208,18 @@
                 send[tile_rows(n, per, 3 * p + t, q), :] = tile
 
 
-def gate_kernel(res, up, zhat, w_gate, w_out, gains, d_out, slope, grad, wgt):
+def gate_kernel(res, up, zhat, w_gate, w_out, gains, d_out, slope, grad, wgt, wo):
     gain0, gain1 = column(gains[0:1, :]), column(gains[1:2, :])
-    wgt[...] = w_gate[...].T
+    wgt[...] = stack_left(w_gate[...].T)
+    wo[...] = stack_left(w_out[...])
 
     def step(c, _):
         at = pl.ds(pl.multiple_of(c * LANES, LANES), LANES)
-        gate = jax.nn.sigmoid(dot3(parts(wgt[...]), parts(zhat[:, at] * gain0)))
+        gate = jax.nn.sigmoid(dot_stacked(wgt[...], stack_rows(zhat[:, at] * gain0)))
         passed = load_cells(up, c, res) * gate
         d_out[:, at] = passed
         slope[:, at] = passed * (1.0 - gate)
-        grad[:, at] = dot3(parts(w_out[...]), parts(passed)) * gain1
+        grad[:, at] = dot_stacked(wo[...], stack_rows(passed)) * gain1
         return 0
 
     lax.fori_loop(0, up.shape[0] // LANES, step, 0)
@@ -224,20 +248,20 @@
     lax.fori_loop(0, xhat.shape[1] // LANES, step, 0)
 
 
-def output_kernel(xhat, zhat, d_out, slope, w_gate, w_out, gains, dzn, mg, mo, wot):
+def output_kernel(xhat, zhat, d_out, slope, w_gate, w_out, gains, dzn, mg, mo, wot, wg):
     gain1 = column(gains[1:2, :])
-    wot[...] = w_out[...].T
+    wot[...] = stack_left(w_out[...].T)
+    wg[...] = stack_left(w_gate[...])
     mg[...] = jnp.zeros_like(mg)
     mo[...] = jnp.zeros_like(mo)
 
     def step(c, _):
         at = pl.ds(pl.multiple_of(c * LANES, LANES), LANES)
         normal = xhat[:, at]
-        out = dot3(parts(wot[...]), parts(normal * gain1))
-        d_logit = parts(slope[:, at] * out)
-        mo[...] += dot3(parts(d_out[:, at]), parts(normal), NT)
-        mg[...] += dot3(d_logit, parts(zhat[:, at]), NT)
-        dzn[:, at] = dot3(parts(w_gate[...]), d_logit)
+        d_logit = stack_rows(slope[:, at] * dot_stacked(wot[...], stack_rows(normal * gain1)))
+        mo[...] += dot_cells(stack_rows(d_out[:, at]), stack_rows(normal))
+        mg[...] += dot_cells(d_logit, stack_rows(zhat[:, at]))
+        dzn[:, at] = dot_stacked(wg[...], d_logit)
         return 0
 
     lax.fori_loop(0, xhat.shape[1] // LANES, step, 0)
@@ -315,16 +339,21 @@
     return d_val, d_val * val[rows, at] * (1.0 - gate)
 
 
-def weight_kernel(n, got, zhat, val, sig, mg, mo, keep, give, mi):
-    hidden = val.shape[0] // 2
+def input_kernel(n, res, got, zhat, zinv, val, sig, dzn, w_in, gains, mg, mo, d_pair, keep, give, mi, w_two):
+    width = zhat.shape[0]
+    w_two[...] = stack_rows(w_in[...])
+    gain0 = column(gains[0:1, :])
     mi[...] = jnp.zeros_like(mi)
 
     def step(c, _):
         at = pl.ds(pl.multiple_of(c * LANES, LANES), LANES)
-        z = parts(zhat[:, at])
-        for which in range(2):
-            for k, grad in enumerate(read_grads(n, got, val, sig, c, which)):
-                mi[pl.ds((2 * which + k) * hidden, hidden), :] += dot3(parts(grad), z, NT)
+        z = zhat[:, at]
+        grads = [grad for which in range(2) for grad in read_grads(n, got, val, sig, c, which)]
+        hi, lo = parts(jnp.concatenate(grads, axis=0))
+        mi[...] += dot_cells(jnp.concatenate([hi, lo], axis=0), stack_rows(z))
+        both = jnp.dot(w_two[...], hi, preferred_element_type=F32)
+        total = both[:width] + both[width:] + jnp.dot(w_two[:width, :], lo, preferred_element_type=F32)
+        store_cells(d_pair, c, res, hat_back((total + dzn[:, at]) * gain0, z, zinv[:, at]))
         return 0
 
     lax.fori_loop(0, zhat.shape[1] // LANES, step, 0)
@@ -332,25 +361,6 @@
     low = mi[pl.ds(0, half), :]
     high = jnp.concatenate([mi[pl.ds(half, mi.shape[0] - half), :], mg[...], mo[...]], axis=0)
     keep[...], give[...] = by_core(low, high)
-
-
-def input_kernel(n, res, got, zhat, zinv, val, sig, dzn, w_in, gains, d_pair, w_hi, w_lo):
-    hidden = val.shape[0] // 2
-    wh, wl = parts(w_in[...])
-    w_hi[...], w_lo[...] = wh, wl
-    gain0 = column(gains[0:1, :])
-
-    def step(c, _):
-        at = pl.ds(pl.multiple_of(c * LANES, LANES), LANES)
-        total = dzn[:, at]
-        for which in range(2):
-            for k, grad in enumerate(read_grads(n, got, val, sig, c, which)):
-                cols = pl.ds((2 * which + k) * hidden, hidden)
-                total += dot3((w_hi[:, cols], w_lo[:, cols]), parts(grad))
-        store_cells(d_pair, c, res, hat_back(total * gain0, zhat[:, at], zinv[:, at]))
-        return 0
-
-    lax.fori_loop(0, d_pair.shape[0] // LANES, step, 0)
 
 
 def finish_kernel(mine, theirs, w_in, w_gate, w_out, gains, d_w_in, d_w_gate, d_w_out, d_gains, m):
@@ -447,7 +457,7 @@
     send, zhat, zinv, val, sig = call(
         functools.partial(project_kernel, n, res),
         [((2 * tiles, 128), F32), (flat, F32), ((1, cells), F32), ((2 * hidden, cells), F32), ((2 * hidden, cells), F32)],
-        [pltpu.VMEM((4 * hidden, width), BF16)] * 2,
+        [pltpu.VMEM((4 * hidden, 3 * width), BF16)],
     )(pair2, w_in, gains)
     got = wide(send)
 
@@ -456,10 +466,11 @@
     d_out, slope, grad = call(
         functools.partial(gate_kernel, res),
         [(flat, F32)] * 3,
-        [pltpu.VMEM((width, width), F32)],
+        [pltpu.VMEM((2 * width, 2 * width), BF16), pltpu.VMEM((2 * hidden, 2 * width), BF16)],
         flops=2 * product,
         moved=4 * cells * width * 5,
     )(up2, zhat, w_gate, w_out, gains)
+    other, d_out = lax.optimization_barrier((other, d_out))
     send, a_all, b_all, pm = call(
         functools.partial(triangle_kernel, n),
         [((tiles, 128), F32), ((per, res // 2, 256), F32), ((per * 512, 128), F32), ((512, 128), F32)],
@@ -487,10 +498,11 @@
     dzn, mg, mo = call(
         output_kernel,
         [(flat, F32), ((width, width), F32), ((width, hidden), F32)],
-        [pltpu.VMEM((width, hidden), F32)],
+        [pltpu.VMEM((2 * width, 2 * hidden), BF16), pltpu.VMEM((2 * width, 2 * width), BF16)],
         flops=4 * product,
         moved=4 * cells * width * 5,
     )(xhat, zhat, d_out, slope, w_gate, w_out, gains)
+    taken, dzn, send = lax.optimization_barrier((taken, dzn, send))
     group = (n * 9, per, 128)
     (send,) = call(add_kernel, [((n * 9, 2 * per, 128), F32)])(
         send.reshape(n * 9, 2 * per, 128), keep.reshape(group), taken.reshape(group)
@@ -498,21 +510,13 @@
     got = wide(send)
 
     half = (4 * hidden + 2 * width) // 2
-    keep, give = call(
-        functools.partial(weight_kernel, n),
-        [((half, width), F32), ((half, width), F32)],
-        [pltpu.VMEM((4 * hidden, width), F32)],
-    )(got, zhat, val, sig, mg, mo)
+    d_pair, keep, give = call(
+        functools.partial(input_kernel, n, res),
+        [((cells, width), F32), ((half, width), F32), ((half, width), F32)],
+        [pltpu.VMEM((4 * hidden, width), F32), pltpu.VMEM((2 * width, 4 * hidden), BF16)],
+    )(got, zhat, zinv, val, sig, dzn, w_in, gains, mg, mo)
     mine = reduce_all(keep, give, n, n_dp)
-    mine, got = lax.optimization_barrier((mine, got))
     theirs = swap_cores(mine, n)
-    (d_pair,) = call(
-        functools.partial(input_kernel, n, res),
-        [((cells, width), F32)],
-        [pltpu.VMEM((width, 4 * hidden), BF16)] * 2,
-        flops=4 * product,
-        moved=4 * cells * width * 7,
-    )(got, zhat, zinv, val, sig, dzn, w_in, gains)
 
     d_w_in, d_w_gate, d_w_out, d_gains = call(
         finish_kernel,

time: 197 us -> 186 us (0.944)
  blocking collectives: 97.3 us -> 151 us
  waiting for transfers between devices: 42.4 us -> 2.15 us
  local copies, waits for them, and re-layouts: 16.9 us -> 2.78 us
  starting transfers between devices: 18.7 us -> 14 us
  Pallas kernels: 19.3 us -> 14.9 us
    all_to_all x5 -> x7, blocking collectives: 97.3 us -> 151 us  [exchange(): return lax.all_to_all(x, axis, 0, 0, tiled=True, axis_index_groups=groups)]
    all_to_all x2 -> x0, waiting for transfers between devices: 39.2 us -> none  [exchange(): return lax.all_to_all(x, axis, 0, 0, tiled=True, axis_index_groups=groups)]
    unnamed x48 -> x18, local copies, waits for them, and re-layouts: 16.1 us -> 2.71 us
    all_to_all x2 -> x0, starting transfers between devices: 7.28 us -> none  [exchange(): return lax.all_to_all(x, axis, 0, 0, tiled=True, axis_index_groups=groups)]
    ppermute x4, starting transfers between devices: 11.4 us -> 14 us  [swap_cores(): return lax.ppermute(x, 'dap', [(i, i ^ 1) for i in range(2 * n)])]
    pallas_call x2 -> x1, Pallas kernels: 5.36 us -> 3.5 us  [shards(): call(functools.partial(input_kernel, n, res), [((cells, width), F32), ((h...]
  transfers between devices with their start and end apart: 6 -> 4, of which waited for: 5 -> 2; matrix products, arithmetic and copies ran while one was open for 0% -> 0% of each run, Pallas kernels for 4% -> 3%
where the time goes in v4:
time: 186 us; the launch traced here: 185 us
  blocking collectives  151 us (81%)
  Pallas kernels  14.9 us (8%)
  starting transfers between devices  14 us (8%)
  local copies, waits for them, and re-layouts  2.78 us (1%)
  waiting for transfers between devices  2.15 us (1%)
    all_to_all x7, blocking collectives, exchange(): return lax.all_to_all(x, axis, 0, 0, tiled=True, axis_index_groups=groups)  151 us
    ppermute x4, starting transfers between devices, swap_cores(): return lax.ppermute(x, 'dap', [(i, i ^ 1) for i in range(2 * n)])  14 us
  transfers between devices with their start and end apart: 4, of which 2 were waited for; matrix products, arithmetic and copies ran while one was open for 0% of the time, Pallas kernels for 3%

profile of v4, /device:TPU:1, one launch (start us, length us, event | category | flops | bytes accessed | tf_op | source)
XLA Modules:
  0.0 185.4 jit_solution(6768741795995655811)
XLA Ops:
  0.6 0.0 copy-start
  0.6 0.9 copy-done
  1.6 0.0 copy-start.4
  1.6 1.1 copy-done.4
  2.6 0.0 copy-start.6
  2.7 0.7 copy-done.6
  3.3 2.1 %shard_map.110 = (f32[2304,128]{1,0:T(8,128)S(1)}, f32[128,1152]{1,0:T(8,128)S(1)}, f32[1,1152]{1,0:T(1,128)S(1)}, f32[256,1152]{1,0:T(8,128)S(1)}, f32[256,1152]{1,0:T(8,128)S(1)}) custom-call(f32[1152,128]{1,0:T(8,128)S(1)} %bitcast.32, f32[128,512]{1,0:T(8,128)S(1)} %copy-done, f32[2,128]{1,0:T(2,128)S(1)} %copy-done.6), custom_call_target="tpu_custom_call" | custom-call | tf_op jit(solution)/shard_map/pallas_call | solution.py:457
  5.5 41.5 %all_to_all.35 = f32[16,144,128]{2,1,0:T(8,128)S(1)} all-to-all(f32[16,144,128]{2,1,0:T(8,128)S(1)} %bitcast.27), channel_id=1, replica_groups={{0,2,4,6,8,10,12,14,16,18,20,22,24,26,28,30},{1,3,5,7,9,11,13,15,17,19,..., dimensions={0} | all-to-all | bytes 2359296 | tf_op jit(solution)/shard_map/all_to_all | solution.py:388
  47.0 0.0 copy-start.2
  47.0 0.0 copy-start.3
  47.0 0.0 copy-start.5
  47.0 0.0 copy-start.7
  47.0 0.0 copy-start.8
  47.0 4.3 %collective-permute-start = (f32[1152,128]{1,0:T(8,128)S(1)}, f32[1152,128]{1,0:T(8,128)S(1)}, u32[]{:S(2)}, u32[]{:S(2)}) collective-permute-start(f32[1152,128]{1,0:T(8,128)S(1)} %slice_bitcast_fusion), channel_id=1, source_target_pairs={{0,1},{1,0},{2,3},{3,2},{4,5},{5,4},{6,7},{7,6},{8,9},{9,8},{10,11... | collective-permute-start | bytes 1769480 | tf_op jit(solution)/shard_map/ppermute | solution.py:392
  51.3 0.0 copy-done.2
  51.3 0.0 copy-done.3
  51.3 0.0 copy-done.5
  51.3 0.0 copy-done.7
  51.3 1.7 shard_map.111
  53.1 0.0 collective-permute-done.other
  53.1 0.0 copy-done.8
  53.1 1.7 shard_map.112
  54.8 21.0 %all_to_all.36 = f32[16,72,128]{2,1,0:T(8,128)S(1)} all-to-all(f32[16,72,128]{2,1,0:T(8,128)S(1)} %bitcast.34), channel_id=1, replica_groups={{0,2,4,6,8,10,12,14,16,18,20,22,24,26,28,30},{1,3,5,7,9,11,13,15,17,19,..., dimensions={0} | all-to-all | bytes 1179648 | tf_op jit(solution)/shard_map/all_to_all | solution.py:388
  75.8 0.4 shard_map.113
  76.2 21.0 %all_to_all.37 = f32[16,72,128]{2,1,0:T(8,128)S(1)} all-to-all(f32[16,72,128]{2,1,0:T(8,128)S(1)} %bitcast.35), channel_id=1, replica_groups={{0,2,4,6,8,10,12,14,16,18,20,22,24,26,28,30},{1,3,5,7,9,11,13,15,17,19,..., dimensions={0} | all-to-all | bytes 1179648 | tf_op jit(solution)/shard_map/all_to_all | solution.py:388
  97.2 1.4 shard_map.114
  98.6 4.3 %collective-permute-start.1 = (f32[1152,128]{1,0:T(8,128)S(1)}, f32[1152,128]{1,0:T(8,128)S(1)}, u32[]{:S(2)}, u32[]{:S(2)}) collective-permute-start(f32[1152,128]{1,0:T(8,128)S(1)} %get-tuple-element.52), channel_id=1, source_target_pairs={{0,1},{1,0},{2,3},{3,2},{4,5},{5,4},{6,7},{7,6},{8,9},{9,8},{10,11... | collective-permute-start | bytes 1769480 | tf_op jit(solution)/shard_map/ppermute | solution.py:392
  102.9 1.1 shard_map.116
  104.0 1.9 %shard_map.115 = (f32[128,1152]{1,0:T(8,128)S(1)}, f32[128,128]{1,0:T(8,128)S(1)}, f32[128,128]{1,0:T(8,128)S(1)}) custom-call(f32[128,1152]{1,0:T(8,128)S(1)} %get-tuple-element.53.xhat, f32[128,1152]{1,0:T(8,128)S(1)} %get-tuple-element.42.zhat, f32[128,1152]{1,0:T(8,128)S(1)} %get-tuple-element.54.d_out, f32[128,1152]{1,0:T(8,128)S(1)} %get-tuple-element.55.slope, ...), custom_call_target="tpu_custom_call" | custom-call | flops 452984832 | bytes 2949120 | tf_op jit(solution)/shard_map/pallas_call | solution.py:498
  105.8 0.0 collective-permute-done.1
  105.9 0.1 shard_map.117
  106.0 0.0 copy-start.1
  106.0 35.6 %all_to_all.38 = f32[16,144,128]{2,1,0:T(8,128)S(1)} all-to-all(f32[16,144,128]{2,1,0:T(8,128)S(1)} %bitcast.24), channel_id=1, replica_groups={{0,2,4,6,8,10,12,14,16,18,20,22,24,26,28,30},{1,3,5,7,9,11,13,15,17,19,..., dimensions={0} | all-to-all | bytes 2359296 | tf_op jit(solution)/shard_map/all_to_all | solution.py:388
  141.6 0.0 copy-done.1
  141.6 3.5 %shard_map.118 = (f32[1152,128]{1,0:T(8,128)}, f32[384,128]{1,0:T(8,128)S(1)}, f32[384,128]{1,0:T(8,128)S(1)}) custom-call(f32[2304,128]{1,0:T(8,128)S(1)} %bitcast.23, f32[128,1152]{1,0:T(8,128)S(1)} %get-tuple-element.42.zhat, f32[1,1152]{1,0:T(1,128)S(1)} %get-tuple-element.62.zinv, f32[256,1152]{1,0:T(8,128)S(1)} %get-tuple-element.63.val, ...), custom_call_target="tpu_custom_call" | custom-call | tf_op jit(solution)/shard_map/pallas_call | solution.py:513
  145.1 1.2 collective-permute-start.2
  146.2 1.1 collective-permute-done.2
  147.3 11.2 %all_to_all.39 = f32[16,24,128]{2,1,0:T(8,128)S(1)} all-to-all(f32[16,24,128]{2,1,0:T(8,128)S(1)} %bitcast.36), channel_id=1, replica_groups={{0,8,16,24,32,40,48,56,64,72,80,88,96,104,112,120},{1,9,17,25,33,41,49,..., dimensions={0} | all-to-all | bytes 393216 | tf_op jit(solution)/shard_map/all_to_all | solution.py:388
  158.5 10.2 %all_to_all.40 = f32[8,24,128]{2,1,0:T(8,128)S(1)} all-to-all(f32[8,24,128]{2,1,0:T(8,128)S(1)} %broadcast_in_dim.4), channel_id=1, replica_groups={{0,128,2,130,4,132,6,134},{1,129,3,131,5,133,7,135},{8,136,10,138,12,14..., dimensions={0} | all-to-all | bytes 196608 | tf_op jit(solution)/shard_map/all_to_all | solution.py:388
  168.8 10.3 %all_to_all.41 = f32[16,24,128]{2,1,0:T(8,128)S(1)} all-to-all(f32[16,24,128]{2,1,0:T(8,128)S(1)} %broadcast_in_dim.5), channel_id=1, replica_groups={{0,8,16,24,32,40,48,56,64,72,80,88,96,104,112,120},{1,9,17,25,33,41,49,..., dimensions={0} | all-to-all | bytes 393216 | tf_op jit(solution)/shard_map/all_to_all | solution.py:388
  179.1 4.3 %collective-permute-start.3 = (f32[384,128]{1,0:T(8,128)S(1)}, f32[384,128]{1,0:T(8,128)S(1)}, u32[]{:S(2)}, u32[]{:S(2)}) collective-permute-start(f32[384,128]{1,0:T(8,128)S(1)} %bitcast.28), channel_id=1, source_target_pairs={{0,1},{1,0},{2,3},{3,2},{4,5},{5,4},{6,7},{7,6},{8,9},{9,8},{10,11... | collective-permute-start | bytes 589832 | tf_op jit(solution)/shard_map/ppermute | solution.py:392
  183.4 1.1 collective-permute-done.3.theirs
  184.4 1.0 shard_map.119
  (6 shorter events, 0.1 us)
Async XLA Ops:
  0.6 1.0 copy-start
  1.6 1.1 copy-start.4
  2.6 0.7 copy-start.6
  47.0 4.3 %copy-start.2 = (f32[128,128]{1,0:T(8,128)S(1)}, f32[128,128]{1,0:T(8,128)}, u32[]{:S(2)}) copy-start(f32[128,128]{1,0:T(8,128)} %w_gate.5) | copy-start | bytes 196612
  47.0 4.3 %copy-start.3 = (f32[128,128]{1,0:T(8,128)S(1)}, f32[128,128]{1,0:T(8,128)}, u32[]{:S(2)}) copy-start(f32[128,128]{1,0:T(8,128)} %w_out.5) | copy-start | bytes 196612
  47.0 4.3 %copy-start.5 = (f32[1,6,192,128]{3,2,1,0:T(8,128)S(1)}, f32[1,6,192,128]{3,2,1,0:T(8,128)}, u32[]{:S(2)}) copy-start(f32[1,6,192,128]{3,2,1,0:T(8,128)} %param.8) | copy-start | bytes 1769476
  47.0 4.3 %copy-start.7 = (f32[2,128]{1,0:T(2,128)S(1)}, f32[2,128]{1,0:T(2,128)}, u32[]{:S(2)}) copy-start(f32[2,128]{1,0:T(2,128)} %gains.9) | copy-start | bytes 3076
  47.0 6.1 %copy-start.8 = (s32[1,192]{1,0:T(1,128)S(1)}, s32[1,192]{1,0:T(1,128)}, u32[]{:S(2)}) copy-start(s32[1,192]{1,0:T(1,128)} %mask.1) | copy-start | bytes 2308
  47.0 6.0 %collective-permute-start = (f32[1152,128]{1,0:T(8,128)S(1)}, f32[1152,128]{1,0:T(8,128)S(1)}, u32[]{:S(2)}, u32[]{:S(2)}) collective-permute-start(f32[1152,128]{1,0:T(8,128)S(1)} %slice_bitcast_fusion), channel_id=1, source_target_pairs={{0,1},{1,0},{2,3},{3,2},{4,5},{5,4},{6,7},{7,6},{8,9},{9,8},{10,11... | collective-permute-start | bytes 1769480 | tf_op jit(solution)/shard_map/ppermute | solution.py:392
  98.6 7.2 %collective-permute-start.1 = (f32[1152,128]{1,0:T(8,128)S(1)}, f32[1152,128]{1,0:T(8,128)S(1)}, u32[]{:S(2)}, u32[]{:S(2)}) collective-permute-start(f32[1152,128]{1,0:T(8,128)S(1)} %get-tuple-element.52), channel_id=1, source_target_pairs={{0,1},{1,0},{2,3},{3,2},{4,5},{5,4},{6,7},{7,6},{8,9},{9,8},{10,11... | collective-permute-start | bytes 1769480 | tf_op jit(solution)/shard_map/ppermute | solution.py:392
  106.0 35.6 %copy-start.1 = (f32[128,512]{1,0:T(8,128)S(1)}, f32[128,512]{1,0:T(8,128)}, u32[]{:S(2)}) copy-start(f32[128,512]{1,0:T(8,128)} %w_in.5) | copy-start | bytes 786436
  145.1 2.2 %collective-permute-start.2 = (f32[384,128]{1,0:T(8,128)S(1)}, f32[384,128]{1,0:T(8,128)S(1)}, u32[]{:S(2)}, u32[]{:S(2)}) collective-permute-start(f32[384,128]{1,0:T(8,128)S(1)} %get-tuple-element.70), channel_id=1, source_target_pairs={{0,1},{1,0},{2,3},{3,2},{4,5},{5,4},{6,7},{7,6},{8,9},{9,8},{10,11... | collective-permute-start | bytes 589832 | tf_op jit(solution)/shard_map/ppermute | solution.py:392
  179.1 5.4 %collective-permute-start.3 = (f32[384,128]{1,0:T(8,128)S(1)}, f32[384,128]{1,0:T(8,128)S(1)}, u32[]{:S(2)}, u32[]{:S(2)}) collective-permute-start(f32[384,128]{1,0:T(8,128)S(1)} %bitcast.28), channel_id=1, source_target_pairs={{0,1},{1,0},{2,3},{3,2},{4,5},{5,4},{6,7},{7,6},{8,9},{9,8},{10,11... | collective-permute-start | bytes 589832 | tf_op jit(solution)/shard_map/ppermute | solution.py:392

commit v5 on v4

--- a/solution.py
+++ b/solution.py
@@ -24,7 +24,11 @@
     def one(a, b):
         return lax.dot_general(a, b, (dims, ((), ())), preferred_element_type=F32)
 
-    return one(ah, bh) + (one(ah, bl) + one(al, bh))
+    if dims == TN:
+        return one(jnp.concatenate([ah, al], axis=0), jnp.concatenate([bh, bh], axis=0)) + one(ah, bl)
+    both = one(jnp.concatenate([ah, al], axis=0), bh)
+    m = ah.shape[0]
+    return both[:m] + (both[m:] + one(ah, bl))
 
 
 NT = ((1,), (1,))
@@ -339,21 +343,15 @@
     return d_val, d_val * val[rows, at] * (1.0 - gate)
 
 
-def input_kernel(n, res, got, zhat, zinv, val, sig, dzn, w_in, gains, mg, mo, d_pair, keep, give, mi, w_two):
-    width = zhat.shape[0]
-    w_two[...] = stack_rows(w_in[...])
-    gain0 = column(gains[0:1, :])
+def weight_kernel(n, got, zhat, val, sig, mg, mo, keep, give, d_hi, d_lo, mi):
     mi[...] = jnp.zeros_like(mi)
 
     def step(c, _):
         at = pl.ds(pl.multiple_of(c * LANES, LANES), LANES)
-        z = zhat[:, at]
         grads = [grad for which in range(2) for grad in read_grads(n, got, val, sig, c, which)]
         hi, lo = parts(jnp.concatenate(grads, axis=0))
-        mi[...] += dot_cells(jnp.concatenate([hi, lo], axis=0), stack_rows(z))
-        both = jnp.dot(w_two[...], hi, preferred_element_type=F32)
-        total = both[:width] + both[width:] + jnp.dot(w_two[:width, :], lo, preferred_element_type=F32)
-        store_cells(d_pair, c, res, hat_back((total + dzn[:, at]) * gain0, z, zinv[:, at]))
+        d_hi[:, at], d_lo[:, at] = hi, lo
+        mi[...] += dot_cells(jnp.concatenate([hi, lo], axis=0), stack_rows(zhat[:, at]))
         return 0
 
     lax.fori_loop(0, zhat.shape[1] // LANES, step, 0)
@@ -361,6 +359,21 @@
     low = mi[pl.ds(0, half), :]
     high = jnp.concatenate([mi[pl.ds(half, mi.shape[0] - half), :], mg[...], mo[...]], axis=0)
     keep[...], give[...] = by_core(low, high)
+
+
+def input_kernel(res, d_hi, d_lo, zhat, zinv, dzn, w_in, gains, d_pair, w_two):
+    width = zhat.shape[0]
+    w_two[...] = stack_rows(w_in[...])
+    gain0 = column(gains[0:1, :])
+
+    def step(c, _):
+        at = pl.ds(pl.multiple_of(c * LANES, LANES), LANES)
+        both = jnp.dot(w_two[...], d_hi[:, at], preferred_element_type=F32)
+        total = both[:width] + both[width:] + jnp.dot(w_two[:width, :], d_lo[:, at], preferred_element_type=F32)
+        store_cells(d_pair, c, res, hat_back((total + dzn[:, at]) * gain0, zhat[:, at], zinv[:, at]))
+        return 0
+
+    lax.fori_loop(0, zhat.shape[1] // LANES, step, 0)
 
 
 def finish_kernel(mine, theirs, w_in, w_gate, w_out, gains, d_w_in, d_w_gate, d_w_out, d_gains, m):
@@ -418,7 +431,7 @@
     return planes, lines
 
 
-def reduce_all(keep, give, n, n_dp):
+def reduce_all(keep, n, n_dp):
     planes, lines = plane_and_line(n, n_dp)
     count, width = keep.shape
 
@@ -429,7 +442,7 @@
         return jnp.broadcast_to(x[None], (pieces,) + x.shape)
 
     in_plane, in_line = len(planes[0]), len(lines[0])
-    mine = summed(keep + swap_cores(give, n), planes, in_plane)
+    mine = summed(keep, planes, in_plane)
     mine = summed(spread(mine, in_line), lines, in_line)
     return exchange(spread(mine, in_plane), BOTH, planes).reshape(count, width)
 
@@ -510,12 +523,21 @@
     got = wide(send)
 
     half = (4 * hidden + 2 * width) // 2
-    d_pair, keep, give = call(
-        functools.partial(input_kernel, n, res),
-        [((cells, width), F32), ((half, width), F32), ((half, width), F32)],
-        [pltpu.VMEM((4 * hidden, width), F32), pltpu.VMEM((2 * width, 4 * hidden), BF16)],
-    )(got, zhat, zinv, val, sig, dzn, w_in, gains, mg, mo)
-    mine = reduce_all(keep, give, n, n_dp)
+    keep, give, d_hi, d_lo = call(
+        functools.partial(weight_kernel, n),
+        [((half, width), F32)] * 2 + [((4 * hidden, cells), BF16)] * 2,
+        [pltpu.VMEM((4 * hidden, width), F32)],
+    )(got, zhat, val, sig, mg, mo)
+    taken = swap_cores(give, n)
+    (d_pair,) = call(
+        functools.partial(input_kernel, res),
+        [((cells, width), F32)],
+        [pltpu.VMEM((2 * width, 4 * hidden), BF16)],
+        flops=4 * product,
+        moved=4 * cells * width * 7,
+    )(d_hi, d_lo, zhat, zinv, dzn, w_in, gains)
+    taken, d_pair = lax.optimization_barrier((taken, d_pair))
+    mine = reduce_all(keep + taken, n, n_dp)
     theirs = swap_cores(mine, n)
 
     d_w_in, d_w_gate, d_w_out, d_gains = call(

time: 186 us -> 185 us (level)
    pallas_call x1 -> x2, Pallas kernels: 3.5 us -> 4.24 us  [the longest x1 2.5 us: shards(): call(functools.partial(input_kernel, res), [((cells, width), F32)], [pltp...]
  transfers between devices with their start and end apart: 4 -> 4, of which waited for: 2 -> 1; matrix products, arithmetic and copies ran while one was open for 0% -> 0% of each run, Pallas kernels for 3% -> 4%
where the time goes in v5:
time: 185 us; the launch traced here: 184 us
  blocking collectives  151 us (82%)
  Pallas kernels  15 us (8%)
  starting transfers between devices  13.8 us (7%)
  local copies, waits for them, and re-layouts  2.78 us (2%)
    all_to_all x7, blocking collectives, exchange(): return lax.all_to_all(x, axis, 0, 0, tiled=True, axis_index_groups=groups)  151 us
    ppermute x4, starting transfers between devices, swap_cores(): return lax.ppermute(x, 'dap', [(i, i ^ 1) for i in range(2 * n)])  13.8 us
  transfers between devices with their start and end apart: 4, of which 1 were waited for; matrix products, arithmetic and copies ran while one was open for 0% of the time, Pallas kernels for 4%

profile of v5, /device:TPU:1, one launch (start us, length us, event | category | flops | bytes accessed | tf_op | source)
XLA Modules:
  0.0 184.4 jit_solution(6215954648712054672)
XLA Ops:
  0.6 0.0 copy-start
  0.6 0.9 copy-done
  1.6 0.0 copy-start.4
  1.6 1.1 copy-done.4
  2.6 0.0 copy-start.6
  2.7 0.7 copy-done.6
  3.3 2.1 %shard_map.110 = (f32[2304,128]{1,0:T(8,128)S(1)}, f32[128,1152]{1,0:T(8,128)S(1)}, f32[1,1152]{1,0:T(1,128)S(1)}, f32[256,1152]{1,0:T(8,128)S(1)}, f32[256,1152]{1,0:T(8,128)S(1)}) custom-call(f32[1152,128]{1,0:T(8,128)S(1)} %bitcast.32, f32[128,512]{1,0:T(8,128)S(1)} %copy-done, f32[2,128]{1,0:T(2,128)S(1)} %copy-done.6), custom_call_target="tpu_custom_call" | custom-call | tf_op jit(solution)/shard_map/pallas_call | solution.py:470
  5.5 41.5 %all_to_all.35 = f32[16,144,128]{2,1,0:T(8,128)S(1)} all-to-all(f32[16,144,128]{2,1,0:T(8,128)S(1)} %bitcast.27), channel_id=1, replica_groups={{0,2,4,6,8,10,12,14,16,18,20,22,24,26,28,30},{1,3,5,7,9,11,13,15,17,19,..., dimensions={0} | all-to-all | bytes 2359296 | tf_op jit(solution)/shard_map/all_to_all | solution.py:401
  47.0 0.0 copy-start.2
  47.0 0.0 copy-start.3
  47.0 0.0 copy-start.5
  47.0 0.0 copy-start.7
  47.0 0.0 copy-start.8
  47.0 4.3 %collective-permute-start = (f32[1152,128]{1,0:T(8,128)S(1)}, f32[1152,128]{1,0:T(8,128)S(1)}, u32[]{:S(2)}, u32[]{:S(2)}) collective-permute-start(f32[1152,128]{1,0:T(8,128)S(1)} %slice_bitcast_fusion), channel_id=1, source_target_pairs={{0,1},{1,0},{2,3},{3,2},{4,5},{5,4},{6,7},{7,6},{8,9},{9,8},{10,11... | collective-permute-start | bytes 1769480 | tf_op jit(solution)/shard_map/ppermute | solution.py:405
  51.3 0.0 copy-done.2
  51.3 0.0 copy-done.3
  51.3 0.0 copy-done.5
  51.3 0.0 copy-done.7
  51.3 1.7 shard_map.111
  53.1 0.0 collective-permute-done.other
  53.1 0.0 copy-done.8
  53.1 1.5 shard_map.112
  54.6 21.0 %all_to_all.36 = f32[16,72,128]{2,1,0:T(8,128)S(1)} all-to-all(f32[16,72,128]{2,1,0:T(8,128)S(1)} %bitcast.34), channel_id=1, replica_groups={{0,2,4,6,8,10,12,14,16,18,20,22,24,26,28,30},{1,3,5,7,9,11,13,15,17,19,..., dimensions={0} | all-to-all | bytes 1179648 | tf_op jit(solution)/shard_map/all_to_all | solution.py:401
  75.6 0.4 shard_map.113
  76.0 21.0 %all_to_all.37 = f32[16,72,128]{2,1,0:T(8,128)S(1)} all-to-all(f32[16,72,128]{2,1,0:T(8,128)S(1)} %bitcast.35), channel_id=1, replica_groups={{0,2,4,6,8,10,12,14,16,18,20,22,24,26,28,30},{1,3,5,7,9,11,13,15,17,19,..., dimensions={0} | all-to-all | bytes 1179648 | tf_op jit(solution)/shard_map/all_to_all | solution.py:401
  97.0 1.2 shard_map.114
  98.2 4.3 %collective-permute-start.1 = (f32[1152,128]{1,0:T(8,128)S(1)}, f32[1152,128]{1,0:T(8,128)S(1)}, u32[]{:S(2)}, u32[]{:S(2)}) collective-permute-start(f32[1152,128]{1,0:T(8,128)S(1)} %get-tuple-element.55), channel_id=1, source_target_pairs={{0,1},{1,0},{2,3},{3,2},{4,5},{5,4},{6,7},{7,6},{8,9},{9,8},{10,11... | collective-permute-start | bytes 1769480 | tf_op jit(solution)/shard_map/ppermute | solution.py:405
  102.5 0.8 shard_map.116
  103.3 1.9 %shard_map.115 = (f32[128,1152]{1,0:T(8,128)S(1)}, f32[128,128]{1,0:T(8,128)S(1)}, f32[128,128]{1,0:T(8,128)S(1)}) custom-call(f32[128,1152]{1,0:T(8,128)S(1)} %get-tuple-element.56.xhat, f32[128,1152]{1,0:T(8,128)S(1)} %get-tuple-element.45.zhat, f32[128,1152]{1,0:T(8,128)S(1)} %get-tuple-element.57.d_out, f32[128,1152]{1,0:T(8,128)S(1)} %get-tuple-element.58.slope, ...), custom_call_target="tpu_custom_call" | custom-call | flops 452984832 | bytes 2949120 | tf_op jit(solution)/shard_map/pallas_call | solution.py:511
  105.2 0.0 collective-permute-done.1
  105.2 0.1 shard_map.117
  105.3 35.4 %all_to_all.38 = f32[16,144,128]{2,1,0:T(8,128)S(1)} all-to-all(f32[16,144,128]{2,1,0:T(8,128)S(1)} %bitcast.23), channel_id=1, replica_groups={{0,2,4,6,8,10,12,14,16,18,20,22,24,26,28,30},{1,3,5,7,9,11,13,15,17,19,..., dimensions={0} | all-to-all | bytes 2359296 | tf_op jit(solution)/shard_map/all_to_all | solution.py:401
  140.7 0.0 copy-start.1
  140.7 1.7 shard_map.118
  142.5 1.3 collective-permute-start.2
  143.7 0.0 copy-done.1
  143.7 2.5 %shard_map.119 = f32[1152,128]{1,0:T(8,128)} custom-call(bf16[512,1152]{1,0:T(8,128)(2,1)S(1)} %get-tuple-element.70.d_hi, bf16[512,1152]{1,0:T(8,128)(2,1)S(1)} %get-tuple-element.71.d_lo, f32[128,1152]{1,0:T(8,128)S(1)} %get-tuple-element.45.zhat, f32[1,1152]{1,0:T(1,128)S(1)} %get-tuple-element.72.zinv, f32[128,1152]{1,0:T(8,128)S(1)} %get-tuple-element.73.dzn, ...), custom_call_target="tpu_custom_call" | custom-call | flops 452984832 | bytes 4128768 | tf_op jit(solution)/shard_map/pallas_call | solution.py:532
  146.2 0.0 collective-permute-done.2
  146.3 11.3 %all_to_all.39 = f32[16,24,128]{2,1,0:T(8,128)S(1)} all-to-all(f32[16,24,128]{2,1,0:T(8,128)S(1)} %bitcast.36), channel_id=1, replica_groups={{0,8,16,24,32,40,48,56,64,72,80,88,96,104,112,120},{1,9,17,25,33,41,49,..., dimensions={0} | all-to-all | bytes 393216 | tf_op jit(solution)/shard_map/all_to_all | solution.py:401
  157.6 10.2 %all_to_all.40 = f32[8,24,128]{2,1,0:T(8,128)S(1)} all-to-all(f32[8,24,128]{2,1,0:T(8,128)S(1)} %broadcast_in_dim.4), channel_id=1, replica_groups={{0,128,2,130,4,132,6,134},{1,129,3,131,5,133,7,135},{8,136,10,138,12,14..., dimensions={0} | all-to-all | bytes 196608 | tf_op jit(solution)/shard_map/all_to_all | solution.py:401
  167.8 10.5 %all_to_all.41 = f32[16,24,128]{2,1,0:T(8,128)S(1)} all-to-all(f32[16,24,128]{2,1,0:T(8,128)S(1)} %broadcast_in_dim.5), channel_id=1, replica_groups={{0,8,16,24,32,40,48,56,64,72,80,88,96,104,112,120},{1,9,17,25,33,41,49,..., dimensions={0} | all-to-all | bytes 393216 | tf_op jit(solution)/shard_map/all_to_all | solution.py:401
  178.3 4.0 %collective-permute-start.3 = (f32[384,128]{1,0:T(8,128)S(1)}, f32[384,128]{1,0:T(8,128)S(1)}, u32[]{:S(2)}, u32[]{:S(2)}) collective-permute-start(f32[384,128]{1,0:T(8,128)S(1)} %bitcast.28), channel_id=1, source_target_pairs={{0,1},{1,0},{2,3},{3,2},{4,5},{5,4},{6,7},{7,6},{8,9},{9,8},{10,11... | collective-permute-start | bytes 589832 | tf_op jit(solution)/shard_map/ppermute | solution.py:405
  182.3 1.1 collective-permute-done.3.theirs
  183.4 1.0 shard_map.120
  (6 shorter events, 0.1 us)
Async XLA Ops:
  0.6 1.0 copy-start
  1.6 1.1 copy-start.4
  2.6 0.7 copy-start.6
  47.0 4.3 %copy-start.2 = (f32[128,128]{1,0:T(8,128)S(1)}, f32[128,128]{1,0:T(8,128)}, u32[]{:S(2)}) copy-start(f32[128,128]{1,0:T(8,128)} %w_gate.5) | copy-start | bytes 196612
  47.0 4.3 %copy-start.3 = (f32[128,128]{1,0:T(8,128)S(1)}, f32[128,128]{1,0:T(8,128)}, u32[]{:S(2)}) copy-start(f32[128,128]{1,0:T(8,128)} %w_out.5) | copy-start | bytes 196612
  47.0 4.3 %copy-start.5 = (f32[1,6,192,128]{3,2,1,0:T(8,128)S(1)}, f32[1,6,192,128]{3,2,1,0:T(8,128)}, u32[]{:S(2)}) copy-start(f32[1,6,192,128]{3,2,1,0:T(8,128)} %param.8) | copy-start | bytes 1769476
  47.0 4.3 %copy-start.7 = (f32[2,128]{1,0:T(2,128)S(1)}, f32[2,128]{1,0:T(2,128)}, u32[]{:S(2)}) copy-start(f32[2,128]{1,0:T(2,128)} %gains.9) | copy-start | bytes 3076
  47.0 6.1 %copy-start.8 = (s32[1,192]{1,0:T(1,128)S(1)}, s32[1,192]{1,0:T(1,128)}, u32[]{:S(2)}) copy-start(s32[1,192]{1,0:T(1,128)} %mask.1) | copy-start | bytes 2308
  47.0 6.0 %collective-permute-start = (f32[1152,128]{1,0:T(8,128)S(1)}, f32[1152,128]{1,0:T(8,128)S(1)}, u32[]{:S(2)}, u32[]{:S(2)}) collective-permute-start(f32[1152,128]{1,0:T(8,128)S(1)} %slice_bitcast_fusion), channel_id=1, source_target_pairs={{0,1},{1,0},{2,3},{3,2},{4,5},{5,4},{6,7},{7,6},{8,9},{9,8},{10,11... | collective-permute-start | bytes 1769480 | tf_op jit(solution)/shard_map/ppermute | solution.py:405
  98.2 7.0 %collective-permute-start.1 = (f32[1152,128]{1,0:T(8,128)S(1)}, f32[1152,128]{1,0:T(8,128)S(1)}, u32[]{:S(2)}, u32[]{:S(2)}) collective-permute-start(f32[1152,128]{1,0:T(8,128)S(1)} %get-tuple-element.55), channel_id=1, source_target_pairs={{0,1},{1,0},{2,3},{3,2},{4,5},{5,4},{6,7},{7,6},{8,9},{9,8},{10,11... | collective-permute-start | bytes 1769480 | tf_op jit(solution)/shard_map/ppermute | solution.py:405
  140.7 3.0 %copy-start.1 = (f32[128,512]{1,0:T(8,128)S(1)}, f32[128,512]{1,0:T(8,128)}, u32[]{:S(2)}) copy-start(f32[128,512]{1,0:T(8,128)} %w_in.5) | copy-start | bytes 786436
  142.5 3.8 %collective-permute-start.2 = (f32[384,128]{1,0:T(8,128)S(1)}, f32[384,128]{1,0:T(8,128)S(1)}, u32[]{:S(2)}, u32[]{:S(2)}) collective-permute-start(f32[384,128]{1,0:T(8,128)S(1)} %get-tuple-element.69), channel_id=1, source_target_pairs={{0,1},{1,0},{2,3},{3,2},{4,5},{5,4},{6,7},{7,6},{8,9},{9,8},{10,11... | collective-permute-start | bytes 589832 | tf_op jit(solution)/shard_map/ppermute | solution.py:405
  178.3 5.1 %collective-permute-start.3 = (f32[384,128]{1,0:T(8,128)S(1)}, f32[384,128]{1,0:T(8,128)S(1)}, u32[]{:S(2)}, u32[]{:S(2)}) collective-permute-start(f32[384,128]{1,0:T(8,128)S(1)} %bitcast.28), channel_id=1, source_target_pairs={{0,1},{1,0},{2,3},{3,2},{4,5},{5,4},{6,7},{7,6},{8,9},{9,8},{10,11... | collective-permute-start | bytes 589832 | tf_op jit(solution)/shard_map/ppermute | solution.py:405

commit v6 on v5

--- a/solution.py
+++ b/solution.py
@@ -86,7 +86,7 @@
 
 
 def cell_slices(c, res):
-    base = pl.multiple_of(c * 2 * res, 2 * res)
+    base = c * 2 * res
     return (
         pl.ds(base, 128),
         pl.ds(base + 128, res - 128),
@@ -127,8 +127,8 @@
     wt[...] = jnp.concatenate([wh, wl, wh], axis=1)
     gain = column(gains[0:1, :])
 
-    def step(c, _):
-        at = pl.ds(pl.multiple_of(c * LANES, LANES), LANES)
+    def step(c):
+        at = pl.ds(c * LANES, LANES)
         z, inverse = hat(load_cells(pair, c, res))
         zhat[:, at] = z
         zinv[:, at] = inverse
@@ -146,9 +146,9 @@
                     send[tile_rows(n, 2 * per, 3 * c + t, which * per + q), :] = both[
                         q * n : (q + 1) * n, t * 128 : (t + 1) * 128
                     ]
-        return 0
-
-    lax.fori_loop(0, pair.shape[0] // LANES, step, 0)
+
+    for c in range(pair.shape[0] // LANES):
+        step(c)
 
 
 def make_masks(mask, line, swap):
@@ -217,23 +217,23 @@
     wgt[...] = stack_left(w_gate[...].T)
     wo[...] = stack_left(w_out[...])
 
-    def step(c, _):
-        at = pl.ds(pl.multiple_of(c * LANES, LANES), LANES)
+    def step(c):
+        at = pl.ds(c * LANES, LANES)
         gate = jax.nn.sigmoid(dot_stacked(wgt[...], stack_rows(zhat[:, at] * gain0)))
         passed = load_cells(up, c, res) * gate
         d_out[:, at] = passed
         slope[:, at] = passed * (1.0 - gate)
         grad[:, at] = dot_stacked(wo[...], stack_rows(passed)) * gain1
-        return 0
-
-    lax.fori_loop(0, up.shape[0] // LANES, step, 0)
+
+    for c in range(up.shape[0] // LANES):
+        step(c)
 
 
 def norm_back_kernel(n, got, grad, send, xhat):
     per = got.shape[0] // (9 * n)
 
-    def step(c, _):
-        at = pl.ds(pl.multiple_of(c * LANES, LANES), LANES)
+    def step(c):
+        at = pl.ds(c * LANES, LANES)
         x = jnp.concatenate(
             [
                 jnp.concatenate([got[tile_rows(n, per, 3 * c + t, q), :] for q in range(per)], axis=0)
@@ -247,9 +247,9 @@
         for q in range(per):
             for t in range(3):
                 send[tile_rows(n, per, 3 * c + t, q), :] = dx[q * n : (q + 1) * n, t * 128 : (t + 1) * 128]
-        return 0
-
-    lax.fori_loop(0, xhat.shape[1] // LANES, step, 0)
+
+    for c in range(xhat.shape[1] // LANES):
+        step(c)
 
 
 def output_kernel(xhat, zhat, d_out, slope, w_gate, w_out, gains, dzn, mg, mo, wot, wg):
@@ -259,16 +259,16 @@
     mg[...] = jnp.zeros_like(mg)
     mo[...] = jnp.zeros_like(mo)
 
-    def step(c, _):
-        at = pl.ds(pl.multiple_of(c * LANES, LANES), LANES)
+    def step(c):
+        at = pl.ds(c * LANES, LANES)
         normal = xhat[:, at]
         d_logit = stack_rows(slope[:, at] * dot_stacked(wot[...], stack_rows(normal * gain1)))
         mo[...] += dot_cells(stack_rows(d_out[:, at]), stack_rows(normal))
         mg[...] += dot_cells(d_logit, stack_rows(zhat[:, at]))
         dzn[:, at] = dot_stacked(wg[...], d_logit)
-        return 0
-
-    lax.fori_loop(0, xhat.shape[1] // LANES, step, 0)
+
+    for c in range(xhat.shape[1] // LANES):
+        step(c)
 
 
 def gather_dx(n, got, q, dx_all):
@@ -329,7 +329,7 @@
 def read_grads(n, got, val, sig, c, which):
     hidden = val.shape[0] // 2
     per = hidden // n
-    at = pl.ds(pl.multiple_of(c * LANES, LANES), LANES)
+    at = pl.ds(c * LANES, LANES)
     d = jnp.concatenate(
         [
             jnp.concatenate([got[tile_rows(n, 2 * per, 3 * c + t, which * per + q), :] for q in range(per)], axis=0)
@@ -346,34 +346,35 @@
 def weight_kernel(n, got, zhat, val, sig, mg, mo, keep, give, d_hi, d_lo, mi):
     mi[...] = jnp.zeros_like(mi)
 
-    def step(c, _):
-        at = pl.ds(pl.multiple_of(c * LANES, LANES), LANES)
+    def step(c):
+        at = pl.ds(c * LANES, LANES)
         grads = [grad for which in range(2) for grad in read_grads(n, got, val, sig, c, which)]
         hi, lo = parts(jnp.concatenate(grads, axis=0))
         d_hi[:, at], d_lo[:, at] = hi, lo
         mi[...] += dot_cells(jnp.concatenate([hi, lo], axis=0), stack_rows(zhat[:, at]))
-        return 0
-
-    lax.fori_loop(0, zhat.shape[1] // LANES, step, 0)
+
+    for c in range(zhat.shape[1] // LANES):
+        step(c)
     half = keep.shape[0]
     low = mi[pl.ds(0, half), :]
     high = jnp.concatenate([mi[pl.ds(half, mi.shape[0] - half), :], mg[...], mo[...]], axis=0)
     keep[...], give[...] = by_core(low, high)
 
 
-def input_kernel(res, d_hi, d_lo, zhat, zinv, dzn, w_in, gains, d_pair, w_two):
+def input_kernel(res, d_hi, d_lo, zhat, zinv, dzn, w_in, gains, d_pair, w_two, rows, sems):
     width = zhat.shape[0]
     w_two[...] = stack_rows(w_in[...])
     gain0 = column(gains[0:1, :])
-
-    def step(c, _):
-        at = pl.ds(pl.multiple_of(c * LANES, LANES), LANES)
+    copies = []
+    for c in range(rows.shape[0] // LANES):
+        at = pl.ds(c * LANES, LANES)
         both = jnp.dot(w_two[...], d_hi[:, at], preferred_element_type=F32)
         total = both[:width] + both[width:] + jnp.dot(w_two[:width, :], d_lo[:, at], preferred_element_type=F32)
-        store_cells(d_pair, c, res, hat_back((total + dzn[:, at]) * gain0, zhat[:, at], zinv[:, at]))
-        return 0
-
-    lax.fori_loop(0, zhat.shape[1] // LANES, step, 0)
+        store_cells(rows, c, res, hat_back((total + dzn[:, at]) * gain0, zhat[:, at], zinv[:, at]))
+        copies.append(pltpu.make_async_copy(rows.at[at, :], d_pair.at[at, :], sems.at[c]))
+        copies[-1].start()
+    for copy in copies:
+        copy.wait()
 
 
 def finish_kernel(mine, theirs, w_in, w_gate, w_out, gains, d_w_in, d_w_gate, d_w_out, d_gains, m):
@@ -395,6 +396,27 @@
     part = m[pl.ds(base + width, width), :].T
     d_w_out[...] = part * gain1
     d_gains[1:2, :] = jnp.sum((part * w_out[...]).T, axis=0, keepdims=True)
+
+
+def input_call(res, cells):
+    def run(*operands):
+        width = operands[2].shape[0]
+        return pl.pallas_call(
+            functools.partial(input_kernel, res),
+            out_shape=[jax.ShapeDtypeStruct((cells, width), F32)],
+            out_specs=[pl.BlockSpec(memory_space=pl.ANY)],
+            scratch_shapes=[
+                pltpu.VMEM((2 * width, operands[0].shape[0]), BF16),
+                pltpu.VMEM((cells, width), F32),
+                pltpu.SemaphoreType.DMA((cells // LANES,)),
+            ],
+            compiler_params=pltpu.CompilerParams(vmem_limit_bytes=16 * 2**20),
+            cost_estimate=pl.CostEstimate(
+                flops=24 * cells * width * width, bytes_accessed=28 * cells * width, transcendentals=0
+            ),
+        )(*operands)
+
+    return run
 
 
 def exchange(x, axis, groups):
@@ -529,13 +551,7 @@
         [pltpu.VMEM((4 * hidden, width), F32)],
     )(got, zhat, val, sig, mg, mo)
     taken = swap_cores(give, n)
-    (d_pair,) = call(
-        functools.partial(input_kernel, res),
-        [((cells, width), F32)],
-        [pltpu.VMEM((2 * width, 4 * hidden), BF16)],
-        flops=4 * product,
-        moved=4 * cells * width * 7,
-    )(d_hi, d_lo, zhat, zinv, dzn, w_in, gains)
+    (d_pair,) = input_call(res, cells)(d_hi, d_lo, zhat, zinv, dzn, w_in, gains)
     taken, d_pair = lax.optimization_barrier((taken, d_pair))
     mine = reduce_all(keep + taken, n, n_dp)
     theirs = swap_cores(mine, n)

time: 185 us -> 183 us (0.989)
  blocking collectives: 151 us -> 155 us
  starting transfers between devices: 13.8 us -> 10.1 us
  Pallas kernels: 15 us -> 12.1 us
    all_to_all x7, blocking collectives: 151 us -> 155 us  [exchange(): return lax.all_to_all(x, axis, 0, 0, tiled=True, axis_index_groups=groups)]
    ppermute x4, starting transfers between devices: 13.8 us -> 10.1 us  [swap_cores(): return lax.ppermute(x, 'dap', [(i, i ^ 1) for i in range(2 * n)])]
  transfers between devices with their start and end apart: 4 -> 4, of which waited for: 1 -> 2; matrix products, arithmetic and copies ran while one was open for 0% -> 0% of each run, Pallas kernels for 4% -> 3%
where the time goes in v6:
time: 183 us; the launch traced here: 182 us
  blocking collectives  155 us (85%)
  Pallas kernels  12.1 us (7%)
  starting transfers between devices  10.1 us (6%)
  local copies, waits for them, and re-layouts  2.78 us (2%)
    all_to_all x7, blocking collectives, exchange(): return lax.all_to_all(x, axis, 0, 0, tiled=True, axis_index_groups=groups)  155 us
    ppermute x4, starting transfers between devices, swap_cores(): return lax.ppermute(x, 'dap', [(i, i ^ 1) for i in range(2 * n)])  10.1 us
  transfers between devices with their start and end apart: 4, of which 2 were waited for; matrix products, arithmetic and copies ran while one was open for 0% of the time, Pallas kernels for 3%

profile of v6, /device:TPU:1, one launch (start us, length us, event | category | flops | bytes accessed | tf_op | source)
XLA Modules:
  0.0 182.2 jit_solution(13796534452323141938)
XLA Ops:
  0.6 0.0 copy-start
  0.6 0.9 copy-done
  1.6 0.0 copy-start.4
  1.6 1.1 copy-done.4
  2.6 0.0 copy-start.6
  2.7 0.7 copy-done.6
  3.3 1.5 shard_map.110
  4.8 41.7 %all_to_all.35 = f32[16,144,128]{2,1,0:T(8,128)S(1)} all-to-all(f32[16,144,128]{2,1,0:T(8,128)S(1)} %bitcast.27), channel_id=1, replica_groups={{0,2,4,6,8,10,12,14,16,18,20,22,24,26,28,30},{1,3,5,7,9,11,13,15,17,19,..., dimensions={0} | all-to-all | bytes 2359296 | tf_op jit(solution)/shard_map/all_to_all | solution.py:423
  46.6 0.0 copy-start.2
  46.6 0.0 copy-start.3
  46.6 0.0 copy-start.5
  46.6 0.0 copy-start.7
  46.6 0.0 copy-start.8
  46.6 4.0 %collective-permute-start = (f32[1152,128]{1,0:T(8,128)S(1)}, f32[1152,128]{1,0:T(8,128)S(1)}, u32[]{:S(2)}, u32[]{:S(2)}) collective-permute-start(f32[1152,128]{1,0:T(8,128)S(1)} %slice_bitcast_fusion), channel_id=1, source_target_pairs={{0,1},{1,0},{2,3},{3,2},{4,5},{5,4},{6,7},{7,6},{8,9},{9,8},{10,11... | collective-permute-start | bytes 1769480 | tf_op jit(solution)/shard_map/ppermute | solution.py:427
  50.7 0.0 copy-done.2
  50.7 0.0 copy-done.3
  50.7 0.0 copy-done.5
  50.7 0.0 copy-done.7
  50.7 1.2 shard_map.111
  51.9 0.4 collective-permute-done.other
  52.3 0.0 copy-done.8
  52.3 1.5 shard_map.112
  53.8 20.8 %all_to_all.36 = f32[16,72,128]{2,1,0:T(8,128)S(1)} all-to-all(f32[16,72,128]{2,1,0:T(8,128)S(1)} %bitcast.34), channel_id=1, replica_groups={{0,2,4,6,8,10,12,14,16,18,20,22,24,26,28,30},{1,3,5,7,9,11,13,15,17,19,..., dimensions={0} | all-to-all | bytes 1179648 | tf_op jit(solution)/shard_map/all_to_all | solution.py:423
  74.6 0.4 shard_map.113
  75.0 24.6 %all_to_all.37 = f32[16,72,128]{2,1,0:T(8,128)S(1)} all-to-all(f32[16,72,128]{2,1,0:T(8,128)S(1)} %bitcast.35), channel_id=1, replica_groups={{0,2,4,6,8,10,12,14,16,18,20,22,24,26,28,30},{1,3,5,7,9,11,13,15,17,19,..., dimensions={0} | all-to-all | bytes 1179648 | tf_op jit(solution)/shard_map/all_to_all | solution.py:423
  99.5 1.2 shard_map.114
  100.7 1.0 collective-permute-start.1
  101.7 0.8 shard_map.116
  102.5 1.2 shard_map.115
  103.8 0.0 collective-permute-done.1
  103.8 0.1 shard_map.117
  103.9 35.1 %all_to_all.38 = f32[16,144,128]{2,1,0:T(8,128)S(1)} all-to-all(f32[16,144,128]{2,1,0:T(8,128)S(1)} %bitcast.23), channel_id=1, replica_groups={{0,2,4,6,8,10,12,14,16,18,20,22,24,26,28,30},{1,3,5,7,9,11,13,15,17,19,..., dimensions={0} | all-to-all | bytes 2359296 | tf_op jit(solution)/shard_map/all_to_all | solution.py:423
  139.0 0.0 copy-start.1
  139.0 1.4 shard_map.118
  140.4 1.1 collective-permute-start.2
  141.5 0.0 copy-done.1
  141.5 1.6 shard_map.119
  143.1 0.0 collective-permute-done.2
  143.2 11.3 %all_to_all.39 = f32[16,24,128]{2,1,0:T(8,128)S(1)} all-to-all(f32[16,24,128]{2,1,0:T(8,128)S(1)} %bitcast.36), channel_id=1, replica_groups={{0,8,16,24,32,40,48,56,64,72,80,88,96,104,112,120},{1,9,17,25,33,41,49,..., dimensions={0} | all-to-all | bytes 393216 | tf_op jit(solution)/shard_map/all_to_all | solution.py:423
  154.6 11.0 %all_to_all.40 = f32[8,24,128]{2,1,0:T(8,128)S(1)} all-to-all(f32[8,24,128]{2,1,0:T(8,128)S(1)} %broadcast_in_dim.4), channel_id=1, replica_groups={{0,128,2,130,4,132,6,134},{1,129,3,131,5,133,7,135},{8,136,10,138,12,14..., dimensions={0} | all-to-all | bytes 196608 | tf_op jit(solution)/shard_map/all_to_all | solution.py:423
  165.6 10.5 %all_to_all.41 = f32[16,24,128]{2,1,0:T(8,128)S(1)} all-to-all(f32[16,24,128]{2,1,0:T(8,128)S(1)} %broadcast_in_dim.5), channel_id=1, replica_groups={{0,8,16,24,32,40,48,56,64,72,80,88,96,104,112,120},{1,9,17,25,33,41,49,..., dimensions={0} | all-to-all | bytes 393216 | tf_op jit(solution)/shard_map/all_to_all | solution.py:423
  176.1 4.0 %collective-permute-start.3 = (f32[384,128]{1,0:T(8,128)S(1)}, f32[384,128]{1,0:T(8,128)S(1)}, u32[]{:S(2)}, u32[]{:S(2)}) collective-permute-start(f32[384,128]{1,0:T(8,128)S(1)} %bitcast.28), channel_id=1, source_target_pairs={{0,1},{1,0},{2,3},{3,2},{4,5},{5,4},{6,7},{7,6},{8,9},{9,8},{10,11... | collective-permute-start | bytes 589832 | tf_op jit(solution)/shard_map/ppermute | solution.py:427
  180.1 1.1 collective-permute-done.3.theirs
  181.2 1.0 shard_map.120
  (6 shorter events, 0.1 us)
Async XLA Ops:
  0.6 1.0 copy-start
  1.6 1.1 copy-start.4
  2.6 0.7 copy-start.6
  46.6 4.1 %copy-start.2 = (f32[128,128]{1,0:T(8,128)S(1)}, f32[128,128]{1,0:T(8,128)}, u32[]{:S(2)}) copy-start(f32[128,128]{1,0:T(8,128)} %w_gate.5) | copy-start | bytes 196612
  46.6 4.1 %copy-start.3 = (f32[128,128]{1,0:T(8,128)S(1)}, f32[128,128]{1,0:T(8,128)}, u32[]{:S(2)}) copy-start(f32[128,128]{1,0:T(8,128)} %w_out.5) | copy-start | bytes 196612
  46.6 4.1 %copy-start.5 = (f32[1,6,192,128]{3,2,1,0:T(8,128)S(1)}, f32[1,6,192,128]{3,2,1,0:T(8,128)}, u32[]{:S(2)}) copy-start(f32[1,6,192,128]{3,2,1,0:T(8,128)} %param.8) | copy-start | bytes 1769476
  46.6 4.1 %copy-start.7 = (f32[2,128]{1,0:T(2,128)S(1)}, f32[2,128]{1,0:T(2,128)}, u32[]{:S(2)}) copy-start(f32[2,128]{1,0:T(2,128)} %gains.9) | copy-start | bytes 3076
  46.6 5.7 %copy-start.8 = (s32[1,192]{1,0:T(1,128)S(1)}, s32[1,192]{1,0:T(1,128)}, u32[]{:S(2)}) copy-start(s32[1,192]{1,0:T(1,128)} %mask.1) | copy-start | bytes 2308
  46.6 5.7 %collective-permute-start = (f32[1152,128]{1,0:T(8,128)S(1)}, f32[1152,128]{1,0:T(8,128)S(1)}, u32[]{:S(2)}, u32[]{:S(2)}) collective-permute-start(f32[1152,128]{1,0:T(8,128)S(1)} %slice_bitcast_fusion), channel_id=1, source_target_pairs={{0,1},{1,0},{2,3},{3,2},{4,5},{5,4},{6,7},{7,6},{8,9},{9,8},{10,11... | collective-permute-start | bytes 1769480 | tf_op jit(solution)/shard_map/ppermute | solution.py:427
  100.7 3.1 %collective-permute-start.1 = (f32[1152,128]{1,0:T(8,128)S(1)}, f32[1152,128]{1,0:T(8,128)S(1)}, u32[]{:S(2)}, u32[]{:S(2)}) collective-permute-start(f32[1152,128]{1,0:T(8,128)S(1)} %get-tuple-element.55), channel_id=1, source_target_pairs={{0,1},{1,0},{2,3},{3,2},{4,5},{5,4},{6,7},{7,6},{8,9},{9,8},{10,11... | collective-permute-start | bytes 1769480 | tf_op jit(solution)/shard_map/ppermute | solution.py:427
  139.0 2.5 %copy-start.1 = (f32[128,512]{1,0:T(8,128)S(1)}, f32[128,512]{1,0:T(8,128)}, u32[]{:S(2)}) copy-start(f32[128,512]{1,0:T(8,128)} %w_in.5) | copy-start | bytes 786436
  140.4 2.8 %collective-permute-start.2 = (f32[384,128]{1,0:T(8,128)S(1)}, f32[384,128]{1,0:T(8,128)S(1)}, u32[]{:S(2)}, u32[]{:S(2)}) collective-permute-start(f32[384,128]{1,0:T(8,128)S(1)} %get-tuple-element.69), channel_id=1, source_target_pairs={{0,1},{1,0},{2,3},{3,2},{4,5},{5,4},{6,7},{7,6},{8,9},{9,8},{10,11... | collective-permute-start | bytes 589832 | tf_op jit(solution)/shard_map/ppermute | solution.py:427
  176.1 5.1 %collective-permute-start.3 = (f32[384,128]{1,0:T(8,128)S(1)}, f32[384,128]{1,0:T(8,128)S(1)}, u32[]{:S(2)}, u32[]{:S(2)}) collective-permute-start(f32[384,128]{1,0:T(8,128)S(1)} %bitcast.28), channel_id=1, source_target_pairs={{0,1},{1,0},{2,3},{3,2},{4,5},{5,4},{6,7},{7,6},{8,9},{9,8},{10,11... | collective-permute-start | bytes 589832 | tf_op jit(solution)/shard_map/ppermute | solution.py:427

commit v7 on v6

--- a/solution.py
+++ b/solution.py
@@ -120,19 +120,18 @@
     return even[0], jnp.where(low, even[1], pltpu.roll(odd[1], 64, 1)), odd[0]
 
 
-def project_kernel(n, res, pair, w_in, gains, send, zhat, zinv, val, sig, wt):
+def project_kernel(n, res, pair, w_in, send, zhat, zinv, val, sig, wt):
     hidden = w_in.shape[1] // 4
     per = hidden // n
     wh, wl = parts(w_in[...].T)
     wt[...] = jnp.concatenate([wh, wl, wh], axis=1)
-    gain = column(gains[0:1, :])
 
     def step(c):
         at = pl.ds(c * LANES, LANES)
         z, inverse = hat(load_cells(pair, c, res))
         zhat[:, at] = z
         zinv[:, at] = inverse
-        zh, zl = parts(z * gain)
+        zh, zl = parts(z)
         zn = jnp.concatenate([zh, zh, zl], axis=0)
         for which in range(2):
             rows = pl.ds(2 * which * hidden, 2 * hidden)
@@ -493,7 +492,7 @@
         functools.partial(project_kernel, n, res),
         [((2 * tiles, 128), F32), (flat, F32), ((1, cells), F32), ((2 * hidden, cells), F32), ((2 * hidden, cells), F32)],
         [pltpu.VMEM((4 * hidden, 3 * width), BF16)],
-    )(pair2, w_in, gains)
+    )(pair2, w_in * gains[0][:, None])
     got = wide(send)
 
     other = swap_cores(got.reshape(n * 9, 2, per, 128)[:, 1].reshape(tiles, 128), n)

time: 183 us -> 182 us (level)
  no operation moved by 1% of the time
where the time goes in v7:
time: 182 us
  blocking collectives  155 us (85%)
  Pallas kernels  11.9 us (7%)
  starting transfers between devices  9.99 us (5%)
  local copies, waits for them, and re-layouts  1.83 us (1%)
    all_to_all x7, blocking collectives, exchange(): return lax.all_to_all(x, axis, 0, 0, tiled=True, axis_index_groups=groups)  155 us
    ppermute x4, starting transfers between devices, swap_cores(): return lax.ppermute(x, 'dap', [(i, i ^ 1) for i in range(2 * n)])  9.99 us
  transfers between devices with their start and end apart: 4, of which 2 were waited for; matrix products, arithmetic and copies ran while one was open for 0% of the time, Pallas kernels for 3%

profile of v7, /device:TPU:1, one launch (start us, length us, event | category | flops | bytes accessed | tf_op | source)
XLA Modules:
  0.0 181.9 jit_solution(4643719359962900741)
XLA Ops:
  0.6 0.7 slice_bitcast_fusion.1
  1.3 1.0 broadcast_multiply_fusion.w_in
  2.4 0.0 copy-start.4
  2.4 1.1 copy-done.4
  3.4 1.4 shard_map.110
  4.8 41.7 %all_to_all.35 = f32[16,144,128]{2,1,0:T(8,128)S(1)} all-to-all(f32[16,144,128]{2,1,0:T(8,128)S(1)} %bitcast.29), channel_id=1, replica_groups={{0,2,4,6,8,10,12,14,16,18,20,22,24,26,28,30},{1,3,5,7,9,11,13,15,17,19,..., dimensions={0} | all-to-all | bytes 2359296 | tf_op jit(solution)/shard_map/all_to_all | solution.py:422
  46.5 0.0 copy-start.1
  46.5 0.0 copy-start.2
  46.5 0.0 copy-start.3
  46.5 0.0 copy-start.5
  46.5 0.0 copy-start.6
  46.6 3.9 %collective-permute-start = (f32[1152,128]{1,0:T(8,128)S(1)}, f32[1152,128]{1,0:T(8,128)S(1)}, u32[]{:S(2)}, u32[]{:S(2)}) collective-permute-start(f32[1152,128]{1,0:T(8,128)S(1)} %slice_bitcast_fusion), channel_id=1, source_target_pairs={{0,1},{1,0},{2,3},{3,2},{4,5},{5,4},{6,7},{7,6},{8,9},{9,8},{10,11... | collective-permute-start | bytes 1769480 | tf_op jit(solution)/shard_map/ppermute | solution.py:426
  50.5 0.0 copy-done.1
  50.5 0.0 copy-done.2
  50.5 0.0 copy-done.3
  50.5 0.0 copy-done.5
  50.5 1.2 shard_map.111
  51.7 0.4 collective-permute-done.other
  52.1 0.0 copy-done.6
  52.1 1.5 shard_map.112
  53.7 20.9 %all_to_all.36 = f32[16,72,128]{2,1,0:T(8,128)S(1)} all-to-all(f32[16,72,128]{2,1,0:T(8,128)S(1)} %bitcast.35), channel_id=1, replica_groups={{0,2,4,6,8,10,12,14,16,18,20,22,24,26,28,30},{1,3,5,7,9,11,13,15,17,19,..., dimensions={0} | all-to-all | bytes 1179648 | tf_op jit(solution)/shard_map/all_to_all | solution.py:422
  74.5 0.4 shard_map.113
  75.0 24.6 %all_to_all.37 = f32[16,72,128]{2,1,0:T(8,128)S(1)} all-to-all(f32[16,72,128]{2,1,0:T(8,128)S(1)} %bitcast.36), channel_id=1, replica_groups={{0,2,4,6,8,10,12,14,16,18,20,22,24,26,28,30},{1,3,5,7,9,11,13,15,17,19,..., dimensions={0} | all-to-all | bytes 1179648 | tf_op jit(solution)/shard_map/all_to_all | solution.py:422
  99.5 1.2 shard_map.114
  100.7 1.0 collective-permute-start.1
  101.7 0.8 shard_map.116
  102.5 1.2 shard_map.115
  103.8 0.0 collective-permute-done.1
  103.8 0.1 shard_map.117
  103.9 35.1 %all_to_all.38 = f32[16,144,128]{2,1,0:T(8,128)S(1)} all-to-all(f32[16,144,128]{2,1,0:T(8,128)S(1)} %bitcast.25), channel_id=1, replica_groups={{0,2,4,6,8,10,12,14,16,18,20,22,24,26,28,30},{1,3,5,7,9,11,13,15,17,19,..., dimensions={0} | all-to-all | bytes 2359296 | tf_op jit(solution)/shard_map/all_to_all | solution.py:422
  139.0 0.0 copy-start
  139.0 1.4 shard_map.118
  140.4 1.1 collective-permute-start.2
  141.5 0.0 copy-done
  141.5 1.6 shard_map.119
  143.1 0.0 collective-permute-done.2
  143.2 11.3 %all_to_all.39 = f32[16,24,128]{2,1,0:T(8,128)S(1)} all-to-all(f32[16,24,128]{2,1,0:T(8,128)S(1)} %bitcast.38), channel_id=1, replica_groups={{0,8,16,24,32,40,48,56,64,72,80,88,96,104,112,120},{1,9,17,25,33,41,49,..., dimensions={0} | all-to-all | bytes 393216 | tf_op jit(solution)/shard_map/all_to_all | solution.py:422
  154.5 10.8 %all_to_all.40 = f32[8,24,128]{2,1,0:T(8,128)S(1)} all-to-all(f32[8,24,128]{2,1,0:T(8,128)S(1)} %broadcast_in_dim.4), channel_id=1, replica_groups={{0,128,2,130,4,132,6,134},{1,129,3,131,5,133,7,135},{8,136,10,138,12,14..., dimensions={0} | all-to-all | bytes 196608 | tf_op jit(solution)/shard_map/all_to_all | solution.py:422
  165.4 10.5 %all_to_all.41 = f32[16,24,128]{2,1,0:T(8,128)S(1)} all-to-all(f32[16,24,128]{2,1,0:T(8,128)S(1)} %broadcast_in_dim.5), channel_id=1, replica_groups={{0,8,16,24,32,40,48,56,64,72,80,88,96,104,112,120},{1,9,17,25,33,41,49,..., dimensions={0} | all-to-all | bytes 393216 | tf_op jit(solution)/shard_map/all_to_all | solution.py:422
  175.9 4.0 %collective-permute-start.3 = (f32[384,128]{1,0:T(8,128)S(1)}, f32[384,128]{1,0:T(8,128)S(1)}, u32[]{:S(2)}, u32[]{:S(2)}) collective-permute-start(f32[384,128]{1,0:T(8,128)S(1)} %bitcast.30), channel_id=1, source_target_pairs={{0,1},{1,0},{2,3},{3,2},{4,5},{5,4},{6,7},{7,6},{8,9},{9,8},{10,11... | collective-permute-start | bytes 589832 | tf_op jit(solution)/shard_map/ppermute | solution.py:426
  179.9 1.1 collective-permute-done.3.theirs
  180.9 1.0 shard_map.120
  (6 shorter events, 0.1 us)
Async XLA Ops:
  2.4 1.1 copy-start.4
  46.5 4.0 %copy-start.1 = (f32[128,128]{1,0:T(8,128)S(1)}, f32[128,128]{1,0:T(8,128)}, u32[]{:S(2)}) copy-start(f32[128,128]{1,0:T(8,128)} %w_gate.5) | copy-start | bytes 196612
  46.5 4.0 %copy-start.2 = (f32[128,128]{1,0:T(8,128)S(1)}, f32[128,128]{1,0:T(8,128)}, u32[]{:S(2)}) copy-start(f32[128,128]{1,0:T(8,128)} %w_out.5) | copy-start | bytes 196612
  46.5 4.0 %copy-start.3 = (f32[1,6,192,128]{3,2,1,0:T(8,128)S(1)}, f32[1,6,192,128]{3,2,1,0:T(8,128)}, u32[]{:S(2)}) copy-start(f32[1,6,192,128]{3,2,1,0:T(8,128)} %param.8) | copy-start | bytes 1769476
  46.5 4.0 %copy-start.5 = (f32[2,128]{1,0:T(2,128)S(1)}, f32[2,128]{1,0:T(2,128)}, u32[]{:S(2)}) copy-start(f32[2,128]{1,0:T(2,128)} %gains.7) | copy-start | bytes 3076
  46.5 5.6 %copy-start.6 = (s32[1,192]{1,0:T(1,128)S(1)}, s32[1,192]{1,0:T(1,128)}, u32[]{:S(2)}) copy-start(s32[1,192]{1,0:T(1,128)} %mask.1) | copy-start | bytes 2308
  46.6 5.6 %collective-permute-start = (f32[1152,128]{1,0:T(8,128)S(1)}, f32[1152,128]{1,0:T(8,128)S(1)}, u32[]{:S(2)}, u32[]{:S(2)}) collective-permute-start(f32[1152,128]{1,0:T(8,128)S(1)} %slice_bitcast_fusion), channel_id=1, source_target_pairs={{0,1},{1,0},{2,3},{3,2},{4,5},{5,4},{6,7},{7,6},{8,9},{9,8},{10,11... | collective-permute-start | bytes 1769480 | tf_op jit(solution)/shard_map/ppermute | solution.py:426
  100.7 3.1 %collective-permute-start.1 = (f32[1152,128]{1,0:T(8,128)S(1)}, f32[1152,128]{1,0:T(8,128)S(1)}, u32[]{:S(2)}, u32[]{:S(2)}) collective-permute-start(f32[1152,128]{1,0:T(8,128)S(1)} %get-tuple-element.55), channel_id=1, source_target_pairs={{0,1},{1,0},{2,3},{3,2},{4,5},{5,4},{6,7},{7,6},{8,9},{9,8},{10,11... | collective-permute-start | bytes 1769480 | tf_op jit(solution)/shard_map/ppermute | solution.py:426
  139.0 2.5 %copy-start = (f32[128,512]{1,0:T(8,128)S(1)}, f32[128,512]{1,0:T(8,128)}, u32[]{:S(2)}) copy-start(f32[128,512]{1,0:T(8,128)} %w_in.3) | copy-start | bytes 786436
  140.4 2.8 %collective-permute-start.2 = (f32[384,128]{1,0:T(8,128)S(1)}, f32[384,128]{1,0:T(8,128)S(1)}, u32[]{:S(2)}, u32[]{:S(2)}) collective-permute-start(f32[384,128]{1,0:T(8,128)S(1)} %get-tuple-element.69), channel_id=1, source_target_pairs={{0,1},{1,0},{2,3},{3,2},{4,5},{5,4},{6,7},{7,6},{8,9},{9,8},{10,11... | collective-permute-start | bytes 589832 | tf_op jit(solution)/shard_map/ppermute | solution.py:426
  175.9 5.1 %collective-permute-start.3 = (f32[384,128]{1,0:T(8,128)S(1)}, f32[384,128]{1,0:T(8,128)S(1)}, u32[]{:S(2)}, u32[]{:S(2)}) collective-permute-start(f32[384,128]{1,0:T(8,128)S(1)} %bitcast.30), channel_id=1, source_target_pairs={{0,1},{1,0},{2,3},{3,2},{4,5},{5,4},{6,7},{7,6},{8,9},{9,8},{10,11... | collective-permute-start | bytes 589832 | tf_op jit(solution)/shard_map/ppermute | solution.py:426
